TPU v7x, 256 devices: a whole 4x4x8 slice. The times are simulated.
256 devices in a mesh: ctx: 16 (over z, x_lo), head: 8 (over x_hi, y), dp: 2 (over core).
Axes of the slice: x: 4 (x_hi: 2, x_lo: 2; x = x_hi * 2 + x_lo), y: 4, z: 8, core: 2. Of those that a mesh axis runs over, the one named last changes fastest.
Arguments:
- queries: bfloat16 [2, 2048, 8192], P('dp', 'ctx', 'head'), may hold values from -16 to 16
- keys: bfloat16 [2, 2048, 1024], P('dp', 'ctx', 'head'), may hold values from -16 to 16
- values: bfloat16 [2, 2048, 1024], P('dp', 'ctx', 'head'), may hold values from -6 to 6
- grad_out: bfloat16 [2, 2048, 8192], P('dp', 'ctx', 'head'), may hold values from -6 to 6
- layer_inputs: bfloat16 [2, 2048, 5120], P('dp', ('ctx', 'head')), may hold values from -24 to 24
- doc_ids: int32 [2, 2048], P('dp'), may hold values from 0 to 7, never falling along the last dimension, each value on 1 to 512 neighbouring positions
- member_rank: int32 [16], replicated, may hold values from -1 to 14, as said below
- take_count: int32 [16], replicated, may hold values from 0 to 32, as said below
Outputs:
- grad_q: bfloat16 [2, 2048, 8192], P('dp', 'ctx', 'head')
- grad_k: bfloat16 [2, 2048, 1024], P('dp', 'ctx', 'head')
- grad_v: bfloat16 [2, 2048, 1024], P('dp', 'ctx', 'head')
- grad_wkv: float32 [5120, 2, 1024], P(('ctx', 'dp'), None, 'head')
Inputs may be any that keep to these rules, and one draw needn't show every extreme that they name: `member_rank`: exactly one block holds -1; the others hold 0 to 14 in block order, skipping it. `take_count`: 0 for the excluded block; the counts sum to 128, and one member takes exactly 32.
All inputs are finite; a program needn't handle non-finite values.
Results may differ from a plain program's by a relative error of at most 0.0052.
Values may be sent and summed in bfloat16 or wider, within the bound.
A program may use at most 64 MiB of HBM per device.

v0:
```python
import math

import jax
import jax.numpy as jnp
from jax import lax
from jax.sharding import PartitionSpec as P

D = 5120
HD = 128


def spread(block, axis, source):
    block = jnp.where(lax.axis_index(axis) == source, block, jnp.zeros_like(block))
    return lax.psum(block, axis)


def passed_along(block, axis, distance):
    devices = range(lax.axis_size(axis))
    route = [(i - distance, i) for i in devices if i - distance in devices]
    return lax.ppermute(block, axis, route)


def block_products(q_rows, g_rows, kv_block, width_k, score_scale):
    ext_rows = kv_block.shape[0]
    local_kv = q_rows.shape[1]
    key_rows = kv_block[:, :width_k].reshape(ext_rows, local_kv, HD)
    value_rows = kv_block[:, width_k:].reshape(ext_rows, local_kv, HD)
    scores = (
        jnp.einsum("iagd,jad->agij", q_rows, key_rows, preferred_element_type=jnp.float32)
        * score_scale
    )
    pushes = jnp.einsum("iagd,jad->agij", g_rows, value_rows, preferred_element_type=jnp.float32)
    return (key_rows, scores, pushes)


def local(queries, keys, values, grad_out, layer_inputs, doc_ids, member_rank, take_count):
    cycle_size = lax.axis_size("ctx")
    block_rows = queries.shape[1]
    spare_rows = block_rows // 4
    ext_rows = block_rows + spare_rows
    width_q = queries.shape[2]
    width_k = keys.shape[2]
    local_kv = width_k // HD
    group_size = width_q // width_k
    score_scale = 1.0 / math.sqrt(HD)
    doc_row = doc_ids[0]
    seq_len = doc_row.shape[0]
    my_index = lax.axis_index("ctx")
    member_indices = jnp.arange(cycle_size, dtype=jnp.int32)
    excluded = jnp.sum(jnp.where(member_rank < 0, member_indices, 0))
    starts = jnp.cumsum(take_count) - take_count
    last_member = cycle_size - 2
    my_slot = member_rank[my_index]
    is_excluded = my_slot < 0
    spare_ids = jnp.arange(spare_rows, dtype=jnp.int32)

    def slot_owner(position):
        clipped = jnp.clip(position, 0, last_member)
        return clipped + (clipped >= excluded).astype(jnp.int32)

    def layout(device):
        own_rows = device * block_rows + jnp.arange(block_rows, dtype=jnp.int32)
        taken_rows = excluded * block_rows + starts[device] + spare_ids
        all_rows = jnp.minimum(jnp.concatenate([own_rows, taken_rows]), seq_len - 1)
        is_live = jnp.concatenate(
            [jnp.ones((block_rows,), dtype=bool), spare_ids < take_count[device]]
        )
        return (all_rows, is_live)

    packed_rows = jnp.concatenate([queries[0], grad_out[0], keys[0], values[0]], 1)
    excluded_block = spread(packed_rows, "ctx", excluded)
    padded_block = jnp.concatenate(
        [excluded_block, jnp.zeros((spare_rows, packed_rows.shape[1]), packed_rows.dtype)], 0
    )
    taken_block = lax.dynamic_slice_in_dim(padded_block, starts[my_index], spare_rows, 0)
    extended = jnp.concatenate([packed_rows, taken_block], 0)
    q_ext = extended[:, :width_q].reshape(ext_rows, local_kv, group_size, HD)
    g_ext = extended[:, width_q : 2 * width_q].reshape(ext_rows, local_kv, group_size, HD)
    kv_ext = extended[:, 2 * width_q :]
    prev_one = slot_owner(my_slot - 1)
    prev_two = slot_owner(my_slot - 2)
    gap_one = my_index - prev_one
    gap_two = my_index - prev_two
    has_one = my_slot >= 1
    has_two = my_slot >= 2
    arrived = []
    carried = kv_ext
    for hop in range(3):
        carried = passed_along(carried, "ctx", 1)
        arrived.append(carried)
    from_near, from_mid, from_far = arrived
    kv_one = jnp.where(gap_one == 1, from_near, from_mid)
    kv_two = jnp.where(gap_two == 2, from_mid, from_far)
    my_rows, my_live = layout(my_index)
    rows_one, live_one = layout(prev_one)
    rows_two, live_two = layout(prev_two)
    my_docs = jnp.take(doc_row, my_rows)

    def visible(key_rows, key_live, present):
        return (
            my_live[:, None]
            & (key_live & present)[None, :]
            & (my_docs[:, None] == jnp.take(doc_row, key_rows)[None, :])
            & (key_rows[None, :] <= my_rows[:, None])
        )

    sources = [
        (kv_ext, visible(my_rows, my_live, True)),
        (kv_one, visible(rows_one, live_one, has_one)),
        (kv_two, visible(rows_two, live_two, has_two)),
    ]
    row_max = jnp.full((local_kv, group_size, ext_rows, 1), -1e30, jnp.float32)
    row_total = jnp.zeros((local_kv, group_size, ext_rows, 1), jnp.float32)
    row_inner = jnp.zeros((local_kv, group_size, ext_rows, 1), jnp.float32)
    kept = []
    for kv_block, mask_rows in sources:
        key_rows, scores, pushes = block_products(q_ext, g_ext, kv_block, width_k, score_scale)
        kept.append((key_rows, scores, pushes, mask_rows))
        new_max = jnp.maximum(
            row_max, jnp.max(jnp.where(mask_rows, scores, -1e30), -1, keepdims=True)
        )
        decay = jnp.exp(row_max - new_max)
        weights = jnp.where(mask_rows, jnp.exp(scores - new_max), 0.0)
        row_total = row_total * decay + jnp.sum(weights, -1, keepdims=True)
        row_inner = row_inner * decay + jnp.sum(weights * pushes, -1, keepdims=True)
        row_max = new_max
    row_total = jnp.where(my_live[:, None], row_total, 1.0)
    row_delta = row_inner / row_total
    grad_q_acc = jnp.zeros((ext_rows, local_kv, group_size, HD), jnp.float32)
    key_parts = []
    for key_rows, scores, pushes, mask_rows in kept:
        prob_rows = jnp.where(mask_rows, jnp.exp(scores - row_max) / row_total, 0.0)
        dscore_b = (prob_rows * (pushes - row_delta)).astype(jnp.bfloat16)
        probs_b = prob_rows.astype(jnp.bfloat16)
        grad_q_acc = grad_q_acc + jnp.einsum(
            "agij,jad->iagd", dscore_b, key_rows, preferred_element_type=jnp.float32
        )
        grad_k_part = (
            jnp.einsum("agij,iagd->jad", dscore_b, q_ext, preferred_element_type=jnp.float32)
            * score_scale
        )
        grad_v_part = jnp.einsum(
            "agij,iagd->jad", probs_b, g_ext, preferred_element_type=jnp.float32
        )
        key_parts.append(
            jnp.concatenate(
                [grad_k_part.reshape(ext_rows, width_k), grad_v_part.reshape(ext_rows, width_k)], 1
            )
        )
    grad_q_ext = (grad_q_acc * score_scale).reshape(ext_rows, width_q)
    own_part, part_one, part_two = key_parts
    next_one = slot_owner(my_slot + 1)
    next_two = slot_owner(my_slot + 2)
    lag_one = next_one - my_index
    lag_two = next_two - my_index
    has_next = (my_slot >= 0) & (my_slot + 1 <= last_member)
    has_after = (my_slot >= 0) & (my_slot + 2 <= last_member)
    returned = []
    carried_back = jnp.stack([part_one, part_two])
    for hop in range(3):
        carried_back = passed_along(carried_back, "ctx", -1)
        returned.append(carried_back)
    from_next = jnp.where(lag_one == 1, returned[0][0], returned[1][0])
    from_after = jnp.where(lag_two == 2, returned[1][1], returned[2][1])
    returned_kv = jnp.where(has_next, from_next, 0.0) + jnp.where(has_after, from_after, 0.0)
    grads_kv = own_part + returned_kv
    take_block = jnp.where(
        (spare_ids < take_count[my_index])[:, None],
        jnp.concatenate([grad_q_ext[block_rows:], grads_kv[block_rows:]], 1),
        0.0,
    ).astype(jnp.bfloat16)
    every_take = lax.all_gather(take_block, "ctx", axis=0, tiled=True)
    positions = jnp.arange(block_rows, dtype=jnp.int32)
    inside = (positions[:, None] >= starts[None, :]) & (
        positions[:, None] < (starts + take_count)[None, :]
    )
    slot_ids = jnp.sum(
        jnp.where(
            inside, member_indices[None, :] * spare_rows + positions[:, None] - starts[None, :], 0
        ),
        1,
    )
    returned_rows = jnp.take(every_take, slot_ids, axis=0)
    own_q = grad_q_ext[:block_rows].astype(jnp.bfloat16)
    own_kv = grads_kv[:block_rows].astype(jnp.bfloat16)
    final_q = jnp.where(is_excluded, returned_rows[:, :width_q], own_q)
    final_kv = jnp.where(is_excluded, returned_rows[:, width_q:], own_kv)
    inputs_full = lax.all_gather(layer_inputs, "head", axis=1, tiled=True)[0]
    rows_mine = D // (cycle_size * lax.axis_size("dp"))
    product = lax.dot_general(
        inputs_full, final_kv, (((0,), (0,)), ((), ())), preferred_element_type=jnp.float32
    )
    grad_w = lax.psum_scatter(
        product.reshape(rows_mine * lax.axis_size(("ctx", "dp")), 2, width_k),
        ("ctx", "dp"),
        scatter_dimension=0,
        tiled=True,
    )
    return (final_q[None], final_kv[:, :width_k][None], final_kv[:, width_k:][None], grad_w)


def solution(mesh):
    in_specs = (
        P("dp", "ctx", "head"),
        P("dp", "ctx", "head"),
        P("dp", "ctx", "head"),
        P("dp", "ctx", "head"),
        P("dp", ("ctx", "head"), None),
        P("dp", None),
        P(),
        P(),
    )
    out_specs = (
        P("dp", "ctx", "head"),
        P("dp", "ctx", "head"),
        P("dp", "ctx", "head"),
        P(("ctx", "dp"), None, "head"),
    )
    return jax.shard_map(local, mesh=mesh, in_specs=in_specs, out_specs=out_specs, check_vma=False)
```

profile of v0, /device:TPU:1, one launch (start us, length us, event | category | flops | bytes accessed | tf_op | source)
XLA Modules:
  0.0 617.7 jit_solution(17842209693417566777)
XLA Ops:
  7.3 1.4 fusion.47
  9.3 2.0 maximum_select_fusion
  11.4 0.6 dynamic_slice.26
  15.6 0.7 fusion.55
  17.1 1.4 gather_fusion.3
  19.2 1.4 gather_fusion.2
  21.3 0.7 iota_compare_fusion.2
  22.6 0.7 iota_compare_fusion.3
  23.3 0.7 iota_compare_fusion.4
  25.1 1.4 gather_fusion.1
  27.8 0.3 compare_and_fusion.2
  28.1 114.8 %all-reduce.8.cloned.1.call-done = bf16[128,2304]{1,0:T(8,128)(2,1)} async-done(((bf16[128,2304]{1,0:T(8,128)(2,1)}), bf16[128,2304]{1,0:T(8,128)(2,1)}) %all-reduce.8.cloned.1.call-update) | async-done | bytes 589840 | tf_op jit(solution)/shard_map/psum | solution.py:14
  142.9 1.0 pad_dynamic-slice_fusion
  144.0 2.1 collective-permute-start
  146.3 1.3 collective-permute-done
  147.6 3.8 collective-permute-start.1
  151.3 0.4 select_reduce_fusion.2
  151.8 1.0 collective-permute-done.1
  152.8 3.7 collective-permute-start.2
  156.5 0.2 fusion.52
  156.8 1.2 collective-permute-done.2
  158.0 0.4 select_reduce_fusion.1
  158.4 0.4 select_reduce_fusion
  158.8 0.5 fusion.13
  159.4 0.5 fusion.14
  159.9 0.5 select_reduce_fusion.3
  160.5 2.4 convert_bitcast_fusion
  162.9 1.4 copy.76
  164.3 2.5 copy.77
  166.8 1.4 copy.78
  168.2 2.1 fusion.10
  170.4 1.5 fusion.8
  171.8 2.5 copy.79
  174.4 1.5 convolution_bitcast_fusion.5
  175.8 1.5 convolution_bitcast_fusion.3
  177.4 0.8 pad_maximum_fusion.2
  178.1 1.3 collective-permute-start.3
  182.8 1.4 copy.75
  184.2 0.4 fusion.57
  184.6 2.6 collective-permute-done.3
  187.3 1.3 collective-permute-start.4
  188.6 0.4 convolution_add_fusion.1
  189.0 0.5 fusion.6
  189.5 7.1 %collective-permute-done.4 = f32[2,160,256]{2,1,0:T(8,128)S(1)} collective-permute-done((f32[2,160,256]{2,1,0:T(8,128)}, f32[2,160,256]{2,1,0:T(8,128)S(1)}, u32[]{:S(2)}, u32[]{:S(2)}) %collective-permute-start.4) | collective-permute-done | bytes 327712 | tf_op jit(solution)/shard_map/ppermute | solution.py:20
  196.6 1.5 collective-permute-start.5
  198.1 0.4 convolution_bitcast_fusion.7
  198.5 0.6 copy.74
  199.1 0.4 fusion.12
  199.5 5.8 collective-permute-done.5
  205.3 1.0 fusion.34
  206.3 0.7 fusion.36
  207.1 0.7 all-gather.5.cloned.1.call-update
  208.6 81.2 %all-gather.3.cloned.1.call-done = bf16[512,1280]{1,0:T(8,128)(2,1)} async-done(((bf16[32,1280]{1,0:T(8,128)(2,1)}), bf16[512,1280]{1,0:T(8,128)(2,1)}) %all-gather.3.cloned.1.call-update) | async-done | bytes 1310736 | tf_op jit(solution)/shard_map/all_gather | solution.py:172
  289.8 2.6 gather_fusion
  292.6 62.2 %all-gather.5.cloned.1.call-done = bf16[1,128,5120]{2,1,0:T(8,128)(2,1)} async-done(((bf16[1,16,5120]{2,1,0:T(8,128)(2,1)}), bf16[1,128,5120]{2,1,0:T(8,128)(2,1)}) %all-gather.5.cloned.1.call-update) | async-done | bytes 1310736 | tf_op jit(solution)/shard_map/all_gather | solution.py:188
  354.9 4.5 fusion.3
  359.4 8.7 %copy.82 = f32[5120,2,128]{2,1,0:T(2,128)} copy(f32[5120,2,128]{0,2,1:T(8,128)} %bitcast.236) | data formatting | bytes 10485760 | tf_op jit(solution)/shard_map/reshape | solution.py:194
  368.1 0.6 copy-done.11
  368.7 0.6 dynamic-slice
  370.0 0.2 copy.80
  370.3 0.6 slice_bitcast_fusion.8
  371.0 0.7 fusion.24
  371.7 237.9 %all-reduce.10.cloned.1.call-done = f32[5120,2,128]{2,1,0:T(2,128)} async-done(((f32[5120,2,128]{2,1,0:T(2,128)}), f32[5120,2,128]{2,1,0:T(2,128)}) %all-reduce.10.cloned.1.call-update) | async-done | bytes 5242896
  609.6 1.6 constant_dynamic-slice_fusion
  (76 shorter events, 1.5 us)
Async XLA Ops:
  7.2 9.9 %copy-start = (s32[1,2048]{1,0:T(1,128)S(1)}, s32[1,2048]{1,0:T(1,128)}, u32[]{:S(2)}) copy-start(s32[1,2048]{1,0:T(1,128)} %param.15) | copy-start | bytes 24580
  7.2 4.2 copy-start.10
  7.2 8.2 %copy-start.9 = (s32[16]{0:T(128)S(1)}, s32[16]{0:T(128)}, u32[]{:S(2)}) copy-start(s32[16]{0:T(128)} %param.17) | copy-start | bytes 196
  7.2 135.7 %all-reduce.8.cloned.1.call-start = ((), (), s32[]{:S(2)}) async-start(), calls=%async_computation | async-start | bytes 1179648 | tf_op jit(solution)/shard_map/psum | solution.py:14
  11.3 278.5 %all-gather.3.cloned.1.call-start = ((), (), s32[]{:S(2)}) async-start(), calls=%async_computation.1 | async-start | bytes 1392640 | tf_op jit(solution)/shard_map/all_gather | solution.py:172
  19.2 124.7 %copy-start.1 = (bf16[1,128,1024]{2,1,0:T(8,128)(2,1)S(1)}, bf16[1,128,1024]{2,1,0:T(8,128)(2,1)}, u32[]{:S(2)}) copy-start(bf16[1,128,1024]{2,1,0:T(8,128)(2,1)} %param.13) | copy-start | bytes 786436
  19.2 124.7 %copy-start.2 = (bf16[1,128,1024]{2,1,0:T(8,128)(2,1)S(1)}, bf16[1,128,1024]{2,1,0:T(8,128)(2,1)}, u32[]{:S(2)}) copy-start(bf16[1,128,1024]{2,1,0:T(8,128)(2,1)} %param.10) | copy-start | bytes 786436
  19.2 124.7 %copy-start.4 = (bf16[1,128,128]{2,1,0:T(8,128)(2,1)S(1)}, bf16[1,128,128]{2,1,0:T(8,128)(2,1)}, u32[]{:S(2)}) copy-start(bf16[1,128,128]{2,1,0:T(8,128)(2,1)} %param.12) | copy-start | bytes 98308
  19.2 124.7 %copy-start.5 = (bf16[1,128,128]{2,1,0:T(8,128)(2,1)S(1)}, bf16[1,128,128]{2,1,0:T(8,128)(2,1)}, u32[]{:S(2)}) copy-start(bf16[1,128,128]{2,1,0:T(8,128)(2,1)} %param.11) | copy-start | bytes 98308
  144.0 3.5 collective-permute-start
  147.6 5.2 collective-permute-start.1
  152.8 5.2 collective-permute-start.2
  158.0 1.4 copy-start.6
  174.4 3.0 copy-start.8
  178.1 9.1 %collective-permute-start.3 = (f32[2,160,256]{2,1,0:T(8,128)}, f32[2,160,256]{2,1,0:T(8,128)}, u32[]{:S(2)}, u32[]{:S(2)}) collective-permute-start(f32[2,160,256]{2,1,0:T(8,128)} %pad_maximum_fusion.2), channel_id=1, source_target_pairs={{16,0},{32,16},{48,32},{64,48},{80,64},{96,80},{112,96},{128,112},... | collective-permute-start | bytes 983048 | tf_op jit(solution)/shard_map/ppermute | solution.py:20
  182.8 5.8 copy-start.7
  187.3 9.4 %collective-permute-start.4 = (f32[2,160,256]{2,1,0:T(8,128)}, f32[2,160,256]{2,1,0:T(8,128)S(1)}, u32[]{:S(2)}, u32[]{:S(2)}) collective-permute-start(f32[2,160,256]{2,1,0:T(8,128)} %collective-permute-done.3), channel_id=1, source_target_pairs={{16,0},{32,16},{48,32},{64,48},{80,64},{96,80},{112,96},{128,112},... | collective-permute-start | bytes 983048 | tf_op jit(solution)/shard_map/ppermute | solution.py:20
  189.0 9.1 %copy-start.3 = (bf16[8,160,160]{2,0,1:T(8,128)(2,1)S(1)}, bf16[8,160,160]{2,0,1:T(8,128)(2,1)}, u32[]{:S(2)}) copy-start(bf16[8,160,160]{2,0,1:T(8,128)(2,1)} %copy.75) | copy-start | bytes 1228804
  196.6 8.7 %collective-permute-start.5 = (f32[2,160,256]{2,1,0:T(8,128)S(1)}, f32[2,160,256]{2,1,0:T(8,128)S(1)}, u32[]{:S(2)}, u32[]{:S(2)}) collective-permute-start(f32[2,160,256]{2,1,0:T(8,128)S(1)} %collective-permute-done.4), channel_id=1, source_target_pairs={{16,0},{32,16},{48,32},{64,48},{80,64},{96,80},{112,96},{128,112},... | collective-permute-start | bytes 983048 | tf_op jit(solution)/shard_map/ppermute | solution.py:20
  207.1 147.8 %all-gather.5.cloned.1.call-start = ((), (), s32[]{:S(2)}) async-start(), calls=%async_computation.2 | async-start | bytes 1474560 | tf_op jit(solution)/shard_map/all_gather | solution.py:188
  207.8 401.8 %all-reduce.10.cloned.1.call-start = ((), (), s32[]{:S(2)}) async-start(), calls=%async_computation.3 | async-start | bytes 10485760
  368.1 0.7 copy-start.11
Sparse Core Ops, SparseCore 0:
  11.5 131.4 all-reduce.7
  207.2 82.6 all-gather.2
  292.8 62.0 all-gather.4
  368.2 241.3 all-reduce.9
where the time goes:
time: 619 us; the launch traced here: 618 us
  waiting for transfers between devices  516 us (83%)
  local copies, waits for them, and re-layouts  32 us (5%)
  between operations  28 us (5%)
  matrix products  15.9 us (3%)
  starting transfers between devices  13.7 us (2%)
  other arithmetic  12 us (2%)
    unnamed x5, waiting for transfers between devices  239 us
    psum x1, waiting for transfers between devices, spread(): return lax.psum(block, axis)  115 us
    all_gather x1, waiting for transfers between devices, local(): every_take = lax.all_gather(take_block, 'ctx', axis=0, tiled=True)  81.2 us
    all_gather x1, waiting for transfers between devices, local(): inputs_full = lax.all_gather(layer_inputs, 'head', axis=1, tiled=True)[0]  62.2 us
    ppermute x6, waiting for transfers between devices, passed_along(): return lax.ppermute(block, axis, route)  19.1 us
    ppermute x6, starting transfers between devices, passed_along(): return lax.ppermute(block, axis, route)  13.6 us
  transfers between devices with their start and end apart: 10, of which 10 were waited for; matrix products, arithmetic and copies ran while one was open for 3% of the time, Pallas kernels for 0%

commit v1 on v0

v1 whole, which is shorter than its diff:
```python
import math

import jax
import jax.numpy as jnp
from jax import lax
from jax.experimental import pallas as pl
from jax.experimental.pallas import tpu as pltpu
from jax.sharding import PartitionSpec as P

HD = 128
BLK = 128
NCTX = 16
NZ = 8
NY = 4
NH = 8
GROUP = 8
WIN = 640
ROWS = 160
BACK = 4
KEYS = (BACK + 1) * BLK
NEG = -1e30
SCALE = 1.0 / math.sqrt(HD)
MESH = pl.DeviceIdType.MESH


def dot(a, b, dims):
    return lax.dot_general(a, b, (dims, ((), ())), preferred_element_type=jnp.float32)


def kernel(
    q_hbm, k_hbm, v_hbm, g_hbm, x_hbm, doc_ref, rank_ref, take_ref,
    oq_hbm, ok_ref, ov_ref, ow_ref,
    qbuf, gbuf, kall, vall, bias, dsb, pbb, csend, crecv, dq, xall, xt, gall, acc, e1, u2, e2,
    loc_sem, a_send, a_recv, x1_send, x1_recv, x2_send, x2_recv, x3_send, x3_recv,
    c_send, c_recv, d_send, d_recv, e_send, e_recv,
):
    c = lax.axis_index("ctx")
    h = lax.axis_index("head")
    d = lax.axis_index("dp")
    z, xl = c // 2, c % 2
    xh, y = h // NY, h % NY

    def ctx(delta):
        return {"ctx": (c + delta + NCTX) % NCTX}

    def head(dx, dy):
        return {"head": ((xh + dx) % 2) * NY + (y + dy) % NY}

    x_peer = {"ctx": c + 1 - 2 * xl}
    core_peer = {"dp": 1 - d}

    local = []

    def fetch(src, dst):
        copy = pltpu.make_async_copy(src, dst, loc_sem.at[len(local)])
        copy.start()
        local.append(copy)

    fetch(k_hbm, kall.at[pl.ds(0, BLK)])
    fetch(v_hbm, vall.at[pl.ds(0, BLK)])
    for n in range(GROUP):
        fetch(q_hbm.at[:, pl.ds(n * HD, HD)], qbuf.at[pl.ds(n * BLK, BLK)])
        fetch(g_hbm.at[:, pl.ds(n * HD, HD)], gbuf.at[pl.ds(n * BLK, BLK)])
    fetch(x_hbm.at[:, pl.ds(pl.multiple_of(z * WIN, 128), WIN)], xall.at[z, h])

    barrier = pltpu.get_barrier_semaphore()
    peers = [ctx(s) for s in (1, 2, 3, 4, -1, -2, -3, -4, 6, -6, 8)]
    peers += [head(1, 0), head(0, 1), head(0, 2), head(0, 3), core_peer]
    for peer in peers:
        pl.semaphore_signal(barrier, inc=1, device_id=peer, device_id_type=MESH)
    pl.semaphore_wait(barrier, len(peers))

    def push(src, dst, send, recv, peer):
        copy = pltpu.make_async_remote_copy(
            src_ref=src, dst_ref=dst, send_sem=send, recv_sem=recv,
            device_id=peer, device_id_type=MESH,
        )
        copy.start()
        return copy

    a_copies = []
    for j in range(1, BACK + 1):
        rows = pl.ds(j * BLK, BLK)
        i = 2 * (j - 1)
        a_copies.append(push(k_hbm, kall.at[rows], a_send.at[i], a_recv.at[i], ctx(j)))
        a_copies.append(
            push(v_hbm, vall.at[rows], a_send.at[i + 1], a_recv.at[i + 1], ctx(j))
        )
    x1_copies = []
    for s in range(1, NZ):
        there = (z + s) % NZ
        x1_copies.append(
            push(
                x_hbm.at[:, pl.ds(pl.multiple_of(there * WIN, 128), WIN)],
                xall.at[z, h], x1_send.at[s - 1], x1_recv.at[s - 1], ctx(2 * s),
            )
        )

    down = lax.broadcasted_iota(jnp.int32, (BLK, BLK), 0)
    across = lax.broadcasted_iota(jnp.int32, (BLK, BLK), 1)
    excluded = jnp.int32(0)
    end = jnp.int32(0)
    count_down = jnp.zeros((BLK, BLK), jnp.int32)
    count_across = jnp.zeros((BLK, BLK), jnp.int32)
    for b in range(NCTX):
        excluded = excluded + jnp.where(rank_ref[b] < 0, b, 0)
        end = end + take_ref[b]
        count_down = count_down + jnp.where(down >= end, 1, 0)
        count_across = count_across + jnp.where(across >= end, 1, 0)
    taken_down = count_down - jnp.where(count_down > excluded, 1, 0)
    taken_across = count_across - jnp.where(count_across > excluded, 1, 0)
    my_rank = jnp.full((BLK, BLK), rank_ref[c], jnp.int32)
    slot_t = jnp.where(my_rank < 0, taken_across, my_rank)
    doc_t = jnp.broadcast_to(
        doc_ref[:, pl.ds(pl.multiple_of(c * BLK, BLK), BLK)], (BLK, BLK)
    )
    for j in range(BACK + 1):
        b = (c - j + NCTX) % NCTX
        rank = jnp.full((BLK, BLK), rank_ref[b], jnp.int32)
        gap = slot_t - jnp.where(rank < 0, taken_down, rank)
        doc_u = jnp.broadcast_to(
            doc_ref[:, pl.ds(pl.multiple_of(b * BLK, BLK), BLK)], (BLK, BLK)
        ).T
        order = (c * BLK + across) - (b * BLK + down)
        seen = (doc_u == doc_t) & (order >= 0) & (gap >= 0) & (gap <= 2)
        bias[pl.ds(j * BLK, BLK), :] = jnp.where(seen, 0.0, NEG)

    for copy in local:
        copy.wait()
    for copy in a_copies:
        copy.wait_recv()
    for copy in x1_copies:
        copy.wait_recv()
    x2_copies = []
    for i, peer in enumerate([head(1, 0), head(0, 1), head(0, 2), head(0, 3)]):
        x2_copies.append(
            push(xall.at[:, h], xall.at[:, h], x2_send.at[i], x2_recv.at[i], peer)
        )

    def weigh(p, carry):
        cols = pl.ds(pl.multiple_of(p * 2 * BLK, 2 * BLK), 2 * BLK)
        q2, g2 = qbuf[cols, :], gbuf[cols, :]
        hidden = bias[...]
        scores = dot(kall[...], q2, ((1,), (1,))) * SCALE
        scores = scores + jnp.concatenate([hidden, hidden], 1)
        top = jnp.max(scores, 0, keepdims=True)
        weights = jnp.exp(scores - top)
        total = jnp.sum(weights, 0, keepdims=True)
        probs = weights * (1.0 / total)
        pushes = dot(vall[...], g2, ((1,), (1,)))
        delta = jnp.sum(probs * pushes, 0, keepdims=True)
        dsb[:, cols] = (probs * (pushes - delta)).astype(jnp.bfloat16)
        pbb[:, cols] = probs.astype(jnp.bfloat16)
        return carry

    lax.fori_loop(0, GROUP // 2, weigh, 0)

    def key_grads(j):
        rows = pl.ds(j * BLK, BLK)
        grad_k = dot(dsb[rows, :], qbuf[...], ((1,), (0,))) * SCALE
        grad_v = dot(pbb[rows, :], gbuf[...], ((1,), (0,)))
        return grad_k, grad_v

    c_copies = []
    for j in range(BACK, 0, -1):
        grad_k, grad_v = key_grads(j)
        csend[j - 1, :, :HD] = grad_k.astype(jnp.bfloat16)
        csend[j - 1, :, HD:] = grad_v.astype(jnp.bfloat16)
        c_copies.append(
            push(
                csend.at[j - 1], crecv.at[j - 1], c_send.at[j - 1], c_recv.at[j - 1], ctx(-j)
            )
        )
    x2_copies[0].wait_recv()
    other = (1 - xh) * NY + y
    x3_copies = []
    for i in range(NY - 1):
        x3_copies.append(
            push(
                xall.at[:, other], xall.at[:, other],
                x3_send.at[i], x3_recv.at[i], head(0, i + 1),
            )
        )
    own_k, own_v = key_grads(0)

    def query_grads(p, carry):
        cols = pl.ds(pl.multiple_of(p * 2 * BLK, 2 * BLK), 2 * BLK)
        both = dot(dsb[:, cols], kall[...], ((0,), (0,))) * SCALE
        dq[2 * p] = both[:BLK].astype(jnp.bfloat16)
        dq[2 * p + 1] = both[BLK:].astype(jnp.bfloat16)
        return carry

    lax.fori_loop(0, GROUP // 2, query_grads, 0)
    out_copies = []
    for n in range(GROUP):
        copy = pltpu.make_async_copy(
            dq.at[n], oq_hbm.at[:, pl.ds(n * HD, HD)], loc_sem.at[n]
        )
        copy.start()
        out_copies.append(copy)

    for copy in x2_copies[1:]:
        copy.wait_recv()
    for copy in x3_copies:
        copy.wait_recv()

    def flip(s, carry):
        xt[s] = xall[s].reshape(BLK, WIN).T
        return carry

    lax.fori_loop(0, NZ, flip, 0)

    for copy in c_copies:
        copy.wait_recv()
    for j in range(BACK):
        own_k = own_k + crecv[j, :, :HD].astype(jnp.float32)
        own_v = own_v + crecv[j, :, HD:].astype(jnp.float32)
    final_k, final_v = own_k.astype(jnp.bfloat16), own_v.astype(jnp.bfloat16)
    gall[z, :, :HD] = final_k
    gall[z, :, HD:] = final_v
    ok_ref[...] = final_k
    ov_ref[...] = final_v

    def relay(step):
        up, low = (z - step + NZ) % NZ, (z + step) % NZ
        if step < NZ // 2 - 1:
            part_up, part_low = gall.at[up], gall.at[low]
        else:
            part_up = gall.at[up, :, pl.ds(0, HD)]
            part_low = gall.at[low, :, pl.ds(HD, HD)]
        return (
            push(part_up, part_up, d_send.at[0, step], d_recv.at[0, step], ctx(2)),
            push(part_low, part_low, d_send.at[1, step], d_recv.at[1, step], ctx(-2)),
        )

    d_copies = [relay(0)]
    acc[...] = dot(xt[z], gall[z], ((1,), (0,)))
    for step in range(1, NZ // 2 + 1):
        for copy in d_copies[-1]:
            copy.wait_recv()
        if step < NZ // 2:
            d_copies.append(relay(step))
        up, low = (z - step + NZ) % NZ, (z + step) % NZ
        if step < NZ // 2:
            acc[...] += dot(xt[up], gall[up], ((1,), (0,))) + dot(
                xt[low], gall[low], ((1,), (0,))
            )
        else:
            acc[...] += dot(xt[up], gall[up], ((1,), (0,)))

    def part(side, core):
        return pl.ds(pl.multiple_of(side * 2 * ROWS + core * ROWS, 32), ROWS)

    e_copies = []
    for i, side in enumerate((1 - xl, xl)):
        e_copies.append(
            push(acc.at[part(side, 1 - d)], e1.at[i], e_send.at[i], e_recv.at[i], core_peer)
        )
    e_copies[0].wait_recv()
    u2[...] = acc[part(1 - xl, d), :] + e1[0]
    e_copies.append(push(u2, e2, e_send.at[2], e_recv.at[2], x_peer))
    e_copies[1].wait_recv()
    e_copies[2].wait_recv()
    ow_ref[...] = acc[part(xl, d), :] + e1[1] + e2[...]

    for copy in out_copies:
        copy.wait()
    for copy in a_copies + x1_copies + x2_copies + x3_copies + c_copies + e_copies:
        copy.wait_send()
    for pair in d_copies:
        for copy in pair:
            copy.wait_send()


def local(queries, keys, values, grad_out, layer_inputs, doc_ids, member_rank, take_count):
    bf16, f32 = jnp.bfloat16, jnp.float32
    hbm = pl.BlockSpec(memory_space=pl.ANY)
    vmem = pl.BlockSpec(memory_space=pltpu.VMEM)
    smem = pl.BlockSpec(memory_space=pltpu.SMEM)
    dma = pltpu.SemaphoreType.DMA
    grad_q, grad_k, grad_v, grad_w = pl.pallas_call(
        kernel,
        out_shape=[
            jax.ShapeDtypeStruct((BLK, GROUP * HD), bf16),
            jax.ShapeDtypeStruct((BLK, HD), bf16),
            jax.ShapeDtypeStruct((BLK, HD), bf16),
            jax.ShapeDtypeStruct((ROWS, 2 * HD), f32),
        ],
        in_specs=[hbm] * 5 + [vmem, smem, smem],
        out_specs=[hbm, vmem, vmem, vmem],
        scratch_shapes=[
            pltpu.VMEM((GROUP * BLK, HD), bf16),
            pltpu.VMEM((GROUP * BLK, HD), bf16),
            pltpu.VMEM((KEYS, HD), bf16),
            pltpu.VMEM((KEYS, HD), bf16),
            pltpu.VMEM((KEYS, BLK), f32),
            pltpu.VMEM((KEYS, GROUP * BLK), bf16),
            pltpu.VMEM((KEYS, GROUP * BLK), bf16),
            pltpu.VMEM((BACK, BLK, 2 * HD), bf16),
            pltpu.VMEM((BACK, BLK, 2 * HD), bf16),
            pltpu.VMEM((GROUP, BLK, HD), bf16),
            pltpu.VMEM((NZ, NH, BLK // NH, WIN), bf16),
            pltpu.VMEM((NZ, WIN, BLK), bf16),
            pltpu.VMEM((NZ, BLK, 2 * HD), bf16),
            pltpu.VMEM((WIN, 2 * HD), f32),
            pltpu.VMEM((2, ROWS, 2 * HD), f32),
            pltpu.VMEM((ROWS, 2 * HD), f32),
            pltpu.VMEM((ROWS, 2 * HD), f32),
            dma((2 * GROUP + 3,)),
            dma((2 * BACK,)),
            dma((2 * BACK,)),
            dma((NZ - 1,)),
            dma((NZ - 1,)),
            dma((NY,)),
            dma((NY,)),
            dma((NY - 1,)),
            dma((NY - 1,)),
            dma((BACK,)),
            dma((BACK,)),
            dma((2, NZ // 2)),
            dma((2, NZ // 2)),
            dma((3,)),
            dma((3,)),
        ],
        compiler_params=pltpu.CompilerParams(
            collective_id=0, has_side_effects=True, vmem_limit_bytes=40 * 1024 * 1024
        ),
        cost_estimate=pl.CostEstimate(
            flops=1300000000, bytes_accessed=2000000, transcendentals=700000
        ),
    )(
        queries[0], keys[0], values[0], grad_out[0], layer_inputs[0],
        doc_ids, member_rank, take_count,
    )
    return (grad_q[None], grad_k[None], grad_v[None], grad_w.reshape(ROWS, 2, HD))


def solution(mesh):
    in_specs = (
        P("dp", "ctx", "head"),
        P("dp", "ctx", "head"),
        P("dp", "ctx", "head"),
        P("dp", "ctx", "head"),
        P("dp", ("ctx", "head"), None),
        P("dp", None),
        P(),
        P(),
    )
    out_specs = (
        P("dp", "ctx", "head"),
        P("dp", "ctx", "head"),
        P("dp", "ctx", "head"),
        P(("ctx", "dp"), None, "head"),
    )
    return jax.shard_map(local, mesh=mesh, in_specs=in_specs, out_specs=out_specs, check_vma=False)
```

time: 619 us -> 71.8 us (0.12)
  waiting for transfers between devices: 516 us -> 0 us
  Pallas kernels: 0 us -> 63.1 us
  between operations: 28 us -> 0.67 us
  local copies, waits for them, and re-layouts: 32 us -> 7.69 us
  matrix products: 15.9 us -> 0 us
  starting transfers between devices: 13.7 us -> 0 us
  other arithmetic: 12 us -> 0 us
    unnamed x5 -> x0, waiting for transfers between devices: 239 us -> none
    all_gather x2 -> x0, waiting for transfers between devices: 143 us -> none  [the longest x1 81.2 us: local(): every_take = lax.all_gather(take_block, 'ctx', axis=0, tiled=True)]
    psum x1 -> x0, waiting for transfers between devices: 115 us -> none  [spread(): return lax.psum(block, axis)]
    pallas_call x0 -> x1, Pallas kernels: none -> 63.1 us  [local(): pl.pallas_call(kernel, out_shape=[jax.ShapeDtypeStruct((BLK, GROUP * HD),...]
    ppermute x6 -> x0, waiting for transfers between devices: 19.1 us -> none  [passed_along(): return lax.ppermute(block, axis, route)]
    dot_general x16 -> x0, matrix products: 15.9 us -> none  [the longest x1 4.51 us: local(): lax.dot_general(inputs_full, final_kv, (((0,), (0,)), ((), ())), preferre...]
    ppermute x6 -> x0, starting transfers between devices: 13.6 us -> none  [passed_along(): return lax.ppermute(block, axis, route)]
    another operation x7 -> x0, local copies, waits for them, and re-layouts: 9.88 us -> none
  transfers between devices with their start and end apart: 10 -> 0, of which waited for: 10 -> 0; matrix products, arithmetic and copies ran while one was open for 3% -> 0% of each run, Pallas kernels for 0% -> 0%
where the time goes in v1:
time: 71.8 us; the launch traced here: 71.5 us
  Pallas kernels  63.1 us (88%)
  local copies, waits for them, and re-layouts  7.69 us (11%)
    pallas_call x1, Pallas kernels, local(): pl.pallas_call(kernel, out_shape=[jax.ShapeDtypeStruct((BLK, GROUP * HD),...  63.1 us
    unnamed x19, local copies, waits for them, and re-layouts  6.94 us

profile of v1, /device:TPU:1, one launch (start us, length us, event | category | flops | bytes accessed | tf_op | source)
XLA Modules:
  0.0 71.5 jit_solution(3469347016012365291)
XLA Ops:
  0.6 0.0 copy-start.5
  0.6 0.0 copy-start.6
  0.7 0.0 copy-start.7
  0.7 0.7 copy-done.5
  1.3 0.0 copy-done.6
  1.3 0.0 copy-done.7
  1.3 0.0 copy-start
  1.3 0.9 %copy-done = bf16[1,128,1024]{2,1,0:T(8,128)(2,1)S(1)} copy-done((bf16[1,128,1024]{2,1,0:T(8,128)(2,1)S(1)}, bf16[1,128,1024]{2,1,0:T(8,128)(2,1)}, u32[]{:S(2)}) %copy-start) | copy-done | bytes 262168
  2.3 0.0 copy-start.1
  2.3 0.9 %copy-done.1 = bf16[1,128,1024]{2,1,0:T(8,128)(2,1)S(1)} copy-done((bf16[1,128,1024]{2,1,0:T(8,128)(2,1)S(1)}, bf16[1,128,1024]{2,1,0:T(8,128)(2,1)}, u32[]{:S(2)}) %copy-start.1) | copy-done | bytes 262168
  3.2 0.0 copy-start.2
  3.2 0.9 %copy-done.2 = bf16[1,16,5120]{2,1,0:T(8,128)(2,1)S(1)} copy-done((bf16[1,16,5120]{2,1,0:T(8,128)(2,1)S(1)}, bf16[1,16,5120]{2,1,0:T(8,128)(2,1)}, u32[]{:S(2)}) %copy-start.2) | copy-done | bytes 163864
  4.2 0.0 copy-start.3
  4.2 0.8 %copy-done.3 = bf16[1,128,128]{2,1,0:T(8,128)(2,1)S(1)} copy-done((bf16[1,128,128]{2,1,0:T(8,128)(2,1)S(1)}, bf16[1,128,128]{2,1,0:T(8,128)(2,1)}, u32[]{:S(2)}) %copy-start.3) | copy-done | bytes 32792
  4.9 0.0 copy-start.4
  4.9 0.8 %copy-done.4 = bf16[1,128,128]{2,1,0:T(8,128)(2,1)S(1)} copy-done((bf16[1,128,128]{2,1,0:T(8,128)(2,1)S(1)}, bf16[1,128,128]{2,1,0:T(8,128)(2,1)}, u32[]{:S(2)}) %copy-start.4) | copy-done | bytes 32792
  5.7 63.1 %shard_map.111 = (bf16[128,1024]{1,0:T(8,128)(2,1)S(1)}, bf16[128,128]{1,0:T(8,128)(2,1)S(1)}, bf16[128,128]{1,0:T(8,128)(2,1)S(1)}, f32[160,256]{1,0:T(8,128)S(1)}) custom-call(bf16[128,1024]{1,0:T(8,128)(2,1)S(1)} %bitcast.11, bf16[128,128]{1,0:T(8,128)(2,1)S(1)} %bitcast.14, bf16[128,128]{1,0:T(8,128)(2,1)S(1)} %bitcast.15, ...), custom_call_target="tpu_custom_call" | custom-call | flops 1300000000 | bytes 2000000 | tf_op jit(solution)/shard_map/pallas_call | solution.py:281
  68.8 0.7 %reshape.11 = f32[160,2,128]{2,1,0:T(2,128)} reshape(f32[160,256]{1,0:T(8,128)S(1)} %get-tuple-element.11) | data formatting | bytes 327680 | tf_op jit(solution)/shard_map/reshape | solution.py:335
  69.5 0.7 copy.15
  70.2 0.6 copy.16
  70.9 0.6 copy.17
Async XLA Ops:
  0.6 0.7 copy-start.5
  0.6 0.7 copy-start.6
  0.7 0.7 copy-start.7
  1.3 1.0 %copy-start = (bf16[1,128,1024]{2,1,0:T(8,128)(2,1)S(1)}, bf16[1,128,1024]{2,1,0:T(8,128)(2,1)}, u32[]{:S(2)}) copy-start(bf16[1,128,1024]{2,1,0:T(8,128)(2,1)} %param.8) | copy-start | bytes 786436
  2.3 0.9 %copy-start.1 = (bf16[1,128,1024]{2,1,0:T(8,128)(2,1)S(1)}, bf16[1,128,1024]{2,1,0:T(8,128)(2,1)}, u32[]{:S(2)}) copy-start(bf16[1,128,1024]{2,1,0:T(8,128)(2,1)} %param.11) | copy-start | bytes 786436
  3.2 0.9 %copy-start.2 = (bf16[1,16,5120]{2,1,0:T(8,128)(2,1)S(1)}, bf16[1,16,5120]{2,1,0:T(8,128)(2,1)}, u32[]{:S(2)}) copy-start(bf16[1,16,5120]{2,1,0:T(8,128)(2,1)} %param.12) | copy-start | bytes 491524
  4.2 0.8 %copy-start.3 = (bf16[1,128,128]{2,1,0:T(8,128)(2,1)S(1)}, bf16[1,128,128]{2,1,0:T(8,128)(2,1)}, u32[]{:S(2)}) copy-start(bf16[1,128,128]{2,1,0:T(8,128)(2,1)} %param.9) | copy-start | bytes 98308
  4.9 0.8 %copy-start.4 = (bf16[1,128,128]{2,1,0:T(8,128)(2,1)S(1)}, bf16[1,128,128]{2,1,0:T(8,128)(2,1)}, u32[]{:S(2)}) copy-start(bf16[1,128,128]{2,1,0:T(8,128)(2,1)} %param.10) | copy-start | bytes 98308

commit v2 on v1

v2 whole, which is shorter than its diff:
```python
import math

import jax
import jax.numpy as jnp
from jax import lax
from jax.experimental import pallas as pl
from jax.experimental.pallas import tpu as pltpu
from jax.sharding import PartitionSpec as P

HD = 128
BLK = 128
NCTX = 16
NZ = 8
NY = 4
NH = 8
GROUP = 8
WIN = 640
ROWS = 160
BACK = 4
KEYS = (BACK + 1) * BLK
NEG = -1e30
PLACE = (0, 1, 3, 5, 7, 6, 4, 2)
ORDER = (4, 3, 5, 2, 6, 1, 7)
SCALE = 1.0 / math.sqrt(HD)
MESH = pl.DeviceIdType.MESH


def dot(a, b, dims):
    return lax.dot_general(a, b, (dims, ((), ())), preferred_element_type=jnp.float32)


def kernel(
    q_hbm, k_hbm, v_hbm, g_hbm, x_hbm, doc_ref, rank_ref, take_ref,
    oq_ref, ok_ref, ov_ref, ow_ref,
    qbuf, gbuf, xbuf, kall, vall, bias, probs, dsb, pbb, vsend, vrecv, ksend, krecv,
    xall, xt, gv, gk, acc_v, acc_k, e1, u2, e2,
    loc_sem, a_send, a_recv, x1_send, x1_recv, x2_send, x2_recv,
    c_send, c_recv, d_send, d_recv, e_send, e_recv,
):
    c = lax.axis_index("ctx")
    h = lax.axis_index("head")
    d = lax.axis_index("dp")
    z, xl = c // 2, c % 2
    xh, y = h // NY, h % NY

    def ctx(delta):
        return {"ctx": (c + delta + NCTX) % NCTX}

    def head_index(dx, dy):
        return ((xh + dx) % 2) * NY + (y + dy + NY) % NY

    def head(dx, dy):
        return {"head": head_index(dx, dy)}

    x_peer = {"ctx": c + 1 - 2 * xl}
    core_peer = {"dp": 1 - d}

    barrier = pltpu.get_barrier_semaphore()
    peers = [ctx(s) for s in (1, 2, 3, 4, -1, -2, -3, -4, 6, -6, 8)]
    peers += [head(1, 0), head(0, 1), head(0, 2), head(0, 3), core_peer]
    for peer in peers:
        pl.semaphore_signal(barrier, inc=1, device_id=peer, device_id_type=MESH)

    local = []

    def fetch(src, dst):
        copy = pltpu.make_async_copy(src, dst, loc_sem.at[len(local)])
        copy.start()
        local.append(copy)

    fetch(k_hbm, kall.at[pl.ds(0, BLK)])
    fetch(v_hbm, vall.at[pl.ds(0, BLK)])
    fetch(x_hbm, xbuf)
    for n in range(GROUP):
        fetch(q_hbm.at[:, pl.ds(n * HD, HD)], qbuf.at[pl.ds(n * BLK, BLK)])
        fetch(g_hbm.at[:, pl.ds(n * HD, HD)], gbuf.at[pl.ds(n * BLK, BLK)])

    down = lax.broadcasted_iota(jnp.int32, (BLK, BLK), 0)
    across = lax.broadcasted_iota(jnp.int32, (BLK, BLK), 1)
    excluded = jnp.int32(0)
    end = jnp.int32(0)
    count_down = jnp.zeros((BLK, BLK), jnp.int32)
    count_across = jnp.zeros((BLK, BLK), jnp.int32)
    for b in range(NCTX):
        excluded = excluded + jnp.where(rank_ref[b] < 0, b, 0)
        end = end + take_ref[b]
        count_down = count_down + jnp.where(down >= end, 1, 0)
        count_across = count_across + jnp.where(across >= end, 1, 0)
    taken_down = count_down - jnp.where(count_down > excluded, 1, 0)
    taken_across = count_across - jnp.where(count_across > excluded, 1, 0)
    my_rank = jnp.full((BLK, BLK), rank_ref[c], jnp.int32)
    slot_t = jnp.where(my_rank < 0, taken_across, my_rank)
    doc_t = jnp.broadcast_to(
        doc_ref[:, pl.ds(pl.multiple_of(c * BLK, BLK), BLK)], (BLK, BLK)
    )
    for j in range(BACK + 1):
        b = (c - j + NCTX) % NCTX
        rank = jnp.full((BLK, BLK), rank_ref[b], jnp.int32)
        gap = slot_t - jnp.where(rank < 0, taken_down, rank)
        doc_u = jnp.broadcast_to(
            doc_ref[:, pl.ds(pl.multiple_of(b * BLK, BLK), BLK)], (BLK, BLK)
        ).T
        order = (c * BLK + across) - (b * BLK + down)
        seen = (doc_u == doc_t) & (order >= 0) & (gap >= 0) & (gap <= 2)
        bias[pl.ds(j * BLK, BLK), :] = jnp.where(seen, 0.0, NEG)

    for copy in local:
        copy.wait()
    window = xbuf[:, pl.ds(pl.multiple_of(z * WIN, 128), WIN)]
    xall[0, h] = window
    pl.semaphore_wait(barrier, len(peers))

    def push(src, dst, send, recv, peer):
        copy = pltpu.make_async_remote_copy(
            src_ref=src, dst_ref=dst, send_sem=send, recv_sem=recv,
            device_id=peer, device_id_type=MESH,
        )
        copy.start()
        return copy

    a_copies = []
    for kind, held in enumerate((kall, vall)):
        for j in range(BACK, 0, -1):
            a_copies.append(
                push(
                    held.at[pl.ds(0, BLK)], held.at[pl.ds(j * BLK, BLK)],
                    a_send.at[kind, j - 1], a_recv.at[kind, j - 1], ctx(j),
                )
            )
    x1_copies = []
    for s in range(1, NZ):
        there = (z + s) % NZ
        x1_copies.append(
            push(
                xbuf.at[:, pl.ds(pl.multiple_of(there * WIN, 128), WIN)],
                xall.at[PLACE[s], h], x1_send.at[s - 1], x1_recv.at[s - 1], ctx(2 * s),
            )
        )
    x2_copies = []

    def spread(at, peer):
        i = len(x2_copies)
        x2_copies.append(push(xall.at[:, at], xall.at[:, at], x2_send.at[i], x2_recv.at[i], peer))

    for copy in a_copies[:BACK]:
        copy.wait_recv()

    def weigh(p, carry):
        cols = pl.ds(pl.multiple_of(p * 2 * BLK, 2 * BLK), 2 * BLK)
        hidden = bias[...]
        scores = dot(kall[...], qbuf[cols, :], ((1,), (1,))) * SCALE
        scores = scores + jnp.concatenate([hidden, hidden], 1)
        top = jnp.max(scores, 0, keepdims=True)
        weights = jnp.exp(scores - top)
        total = jnp.sum(weights, 0, keepdims=True)
        share = weights * (1.0 / total)
        probs[:, cols] = share
        pbb[:, cols] = share.astype(jnp.bfloat16)
        return carry

    lax.fori_loop(0, GROUP // 2, weigh, 0)
    c_copies = []
    for j in range(BACK, 0, -1):
        grad_v = dot(pbb[pl.ds(j * BLK, BLK), :], gbuf[...], ((1,), (0,)))
        vsend[j - 1] = grad_v.astype(jnp.bfloat16)
        c_copies.append(
            push(
                vsend.at[j - 1], vrecv.at[j - 1],
                c_send.at[0, j - 1], c_recv.at[0, j - 1], ctx(-j),
            )
        )
    own_v = dot(pbb[pl.ds(0, BLK), :], gbuf[...], ((1,), (0,)))

    for copy in x1_copies:
        copy.wait_recv()
    spread(h, head(0, 1))
    spread(h, head(0, -1))
    spread(h, head(1, 0))

    for copy in a_copies[BACK:]:
        copy.wait_recv()

    def differ(p, carry):
        cols = pl.ds(pl.multiple_of(p * 2 * BLK, 2 * BLK), 2 * BLK)
        pushes = dot(vall[...], gbuf[cols, :], ((1,), (1,)))
        share = probs[:, cols]
        delta = jnp.sum(share * pushes, 0, keepdims=True)
        dsb[:, cols] = (share * (pushes - delta)).astype(jnp.bfloat16)
        return carry

    lax.fori_loop(0, GROUP // 2, differ, 0)
    for j in range(BACK, 0, -1):
        grad_k = dot(dsb[pl.ds(j * BLK, BLK), :], qbuf[...], ((1,), (0,))) * SCALE
        ksend[j - 1] = grad_k.astype(jnp.bfloat16)
        c_copies.append(
            push(
                ksend.at[j - 1], krecv.at[j - 1],
                c_send.at[1, j - 1], c_recv.at[1, j - 1], ctx(-j),
            )
        )
    own_k = dot(dsb[pl.ds(0, BLK), :], qbuf[...], ((1,), (0,))) * SCALE

    x2_copies[0].wait_recv()
    spread(head_index(0, -1), head(0, 1))

    d_copies = []

    def collect(kind, own, received, copies, held, out_ref):
        for copy in copies:
            copy.wait_recv()
        for j in range(BACK):
            own = own + received[j].astype(jnp.float32)
        final = own.astype(jnp.bfloat16)
        held[0] = final
        out_ref[...] = final
        for s in ORDER:
            d_copies.append(
                push(
                    held.at[0], held.at[PLACE[s]],
                    d_send.at[kind, s - 1], d_recv.at[kind, s - 1], ctx(2 * s),
                )
            )

    collect(0, own_v, vrecv, c_copies[:BACK], gv, ov_ref)

    def query_grads(p, carry):
        cols = pl.ds(pl.multiple_of(p * 2 * BLK, 2 * BLK), 2 * BLK)
        both = dot(dsb[:, cols], kall[...], ((0,), (0,))) * SCALE
        both = both.astype(jnp.bfloat16)
        oq_ref[:, cols] = jnp.concatenate([both[:BLK], both[BLK:]], 1)
        return carry

    lax.fori_loop(0, GROUP // 2, query_grads, 0)

    x2_copies[2].wait_recv()
    spread(head_index(1, 0), head(0, 1))
    spread(head_index(1, 0), head(0, -1))

    collect(1, own_k, krecv, c_copies[BACK:], gk, ok_ref)

    x2_copies[5].wait_recv()
    spread(head_index(1, 1), head(0, -1))
    for i in (1, 3, 4, 6):
        x2_copies[i].wait_recv()

    for i in range(NZ):
        xt[:, pl.ds(i * BLK, BLK)] = xall[i].reshape(BLK, WIN).T

    e_copies = []

    def reduce_cores(kind, held, acc):
        for copy in d_copies[kind * (NZ - 1) : (kind + 1) * (NZ - 1)]:
            copy.wait_recv()
        product = dot(xt[...], held[...].reshape(NZ * BLK, HD), ((1,), (0,)))
        acc[...] = product.reshape(2, 2, ROWS, HD)
        e_copies.append(
            push(
                acc.at[:, 1 - d], e1.at[kind],
                e_send.at[0, kind], e_recv.at[0, kind], core_peer,
            )
        )
        e_copies[-1].wait_recv()
        u2[kind] = acc[1 - xl, d] + e1[kind, 1 - xl]
        e_copies.append(
            push(
                u2.at[kind], e2.at[kind],
                e_send.at[1, kind], e_recv.at[1, kind], x_peer,
            )
        )

    reduce_cores(0, gv, acc_v)
    reduce_cores(1, gk, acc_k)
    e_copies[1].wait_recv()
    ow_ref[1] = acc_v[xl, d] + e1[0, xl] + e2[0]
    e_copies[3].wait_recv()
    ow_ref[0] = acc_k[xl, d] + e1[1, xl] + e2[1]

    for copy in a_copies + x1_copies + x2_copies + c_copies + d_copies + e_copies:
        copy.wait_send()


def finish(q_ref, k_ref, v_ref, w_ref, oq_ref, ok_ref, ov_ref, ow_ref):
    oq_ref[...] = q_ref[...]
    ok_ref[...] = k_ref[...]
    ov_ref[...] = v_ref[...]
    ow_ref[:, 0, :] = w_ref[0]
    ow_ref[:, 1, :] = w_ref[1]


def local(queries, keys, values, grad_out, layer_inputs, doc_ids, member_rank, take_count):
    bf16, f32 = jnp.bfloat16, jnp.float32
    hbm = pl.BlockSpec(memory_space=pltpu.HBM)
    vmem = pl.BlockSpec(memory_space=pltpu.VMEM)
    smem = pl.BlockSpec(memory_space=pltpu.SMEM)
    dma = pltpu.SemaphoreType.DMA
    grad_q, grad_k, grad_v, grad_w = pl.pallas_call(
        kernel,
        out_shape=[
            jax.ShapeDtypeStruct((BLK, GROUP * HD), bf16),
            jax.ShapeDtypeStruct((BLK, HD), bf16),
            jax.ShapeDtypeStruct((BLK, HD), bf16),
            jax.ShapeDtypeStruct((2, ROWS, HD), f32),
        ],
        in_specs=[hbm] * 5 + [vmem, smem, smem],
        out_specs=[vmem] * 4,
        scratch_shapes=[
            pltpu.VMEM((GROUP * BLK, HD), bf16),
            pltpu.VMEM((GROUP * BLK, HD), bf16),
            pltpu.VMEM((BLK // NH, NZ * WIN), bf16),
            pltpu.VMEM((KEYS, HD), bf16),
            pltpu.VMEM((KEYS, HD), bf16),
            pltpu.VMEM((KEYS, BLK), f32),
            pltpu.VMEM((KEYS, GROUP * BLK), f32),
            pltpu.VMEM((KEYS, GROUP * BLK), bf16),
            pltpu.VMEM((KEYS, GROUP * BLK), bf16),
            pltpu.VMEM((BACK, BLK, HD), bf16),
            pltpu.VMEM((BACK, BLK, HD), bf16),
            pltpu.VMEM((BACK, BLK, HD), bf16),
            pltpu.VMEM((BACK, BLK, HD), bf16),
            pltpu.VMEM((NZ, NH, BLK // NH, WIN), bf16),
            pltpu.VMEM((WIN, NZ * BLK), bf16),
            pltpu.VMEM((NZ, BLK, HD), bf16),
            pltpu.VMEM((NZ, BLK, HD), bf16),
            pltpu.VMEM((2, 2, ROWS, HD), f32),
            pltpu.VMEM((2, 2, ROWS, HD), f32),
            pltpu.VMEM((2, 2, ROWS, HD), f32),
            pltpu.VMEM((2, ROWS, HD), f32),
            pltpu.VMEM((2, ROWS, HD), f32),
            dma((2 * GROUP + 3,)),
            dma((2, BACK)),
            dma((2, BACK)),
            dma((NZ - 1,)),
            dma((NZ - 1,)),
            dma((7,)),
            dma((7,)),
            dma((2, BACK)),
            dma((2, BACK)),
            dma((2, NZ - 1)),
            dma((2, NZ - 1)),
            dma((2, 2)),
            dma((2, 2)),
        ],
        compiler_params=pltpu.CompilerParams(
            collective_id=0, has_side_effects=True, vmem_limit_bytes=60 * 1024 * 1024
        ),
        cost_estimate=pl.CostEstimate(
            flops=1300000000, bytes_accessed=2000000, transcendentals=700000
        ),
    )(
        queries[0], keys[0], values[0], grad_out[0], layer_inputs[0],
        doc_ids, member_rank, take_count,
    )
    grad_q, grad_k, grad_v, grad_w = pl.pallas_call(
        finish,
        out_shape=[
            jax.ShapeDtypeStruct((BLK, GROUP * HD), bf16),
            jax.ShapeDtypeStruct((BLK, HD), bf16),
            jax.ShapeDtypeStruct((BLK, HD), bf16),
            jax.ShapeDtypeStruct((ROWS, 2, HD), f32),
        ],
        in_specs=[vmem] * 4,
        out_specs=[vmem] * 4,
    )(grad_q, grad_k, grad_v, grad_w)
    return (grad_q[None], grad_k[None], grad_v[None], grad_w)


def solution(mesh):
    in_specs = (
        P("dp", "ctx", "head"),
        P("dp", "ctx", "head"),
        P("dp", "ctx", "head"),
        P("dp", "ctx", "head"),
        P("dp", ("ctx", "head"), None),
        P("dp", None),
        P(),
        P(),
    )
    out_specs = (
        P("dp", "ctx", "head"),
        P("dp", "ctx", "head"),
        P("dp", "ctx", "head"),
        P(("ctx", "dp"), None, "head"),
    )
    return jax.shard_map(local, mesh=mesh, in_specs=in_specs, out_specs=out_specs, check_vma=False)
```

time: 71.8 us -> 52.4 us (0.73)
  Pallas kernels: 63.1 us -> 51.6 us
  local copies, waits for them, and re-layouts: 7.69 us -> 0 us
    pallas_call x1, Pallas kernels: 63.1 us -> 49.8 us  [local(): pl.pallas_call(kernel, out_shape=[jax.ShapeDtypeStruct((BLK, GROUP * HD),...]
    unnamed x19 -> x0, local copies, waits for them, and re-layouts: 6.94 us -> none
    pallas_call x0 -> x1, Pallas kernels: none -> 1.82 us  [local(): pl.pallas_call(finish, out_shape=[jax.ShapeDtypeStruct((BLK, GROUP * HD),...]
    reshape x1 -> x0, local copies, waits for them, and re-layouts: 0.75 us -> none  [local(): grad_w.reshape(ROWS, 2, HD)]
where the time goes in v2:
time: 52.4 us; the launch traced here: 52.3 us
  Pallas kernels  51.6 us (98%)
  between operations  0.64 us (1%)
    pallas_call x1, Pallas kernels, local(): pl.pallas_call(kernel, out_shape=[jax.ShapeDtypeStruct((BLK, GROUP * HD),...  49.8 us
    pallas_call x1, Pallas kernels, local(): pl.pallas_call(finish, out_shape=[jax.ShapeDtypeStruct((BLK, GROUP * HD),...  1.82 us

profile of v2, /device:TPU:1, one launch (start us, length us, event | category | flops | bytes accessed | tf_op | source)
XLA Modules:
  0.0 52.3 jit_solution(10851641955278212546)
XLA Ops:
  0.6 49.8 %shard_map.111 = (bf16[128,1024]{1,0:T(8,128)(2,1)}, bf16[128,128]{1,0:T(8,128)(2,1)}, bf16[128,128]{1,0:T(8,128)(2,1)}, f32[2,160,128]{2,1,0:T(8,128)}) custom-call(bf16[128,1024]{1,0:T(8,128)(2,1)} %bitcast.8, bf16[128,128]{1,0:T(8,128)(2,1)} %bitcast.12, bf16[128,128]{1,0:T(8,128)(2,1)} %bitcast.13, bf16[128,1024]{1,0:T(8,128)(2,1)} %bitcast.9, ...), custom_call_target="tpu_custom_call" | custom-call | flops 1300000000 | bytes 2000000 | tf_op jit(solution)/shard_map/pallas_call | solution.py:296
  50.4 1.8 %shard_map.112 = (bf16[128,1024]{1,0:T(8,128)(2,1)}, bf16[128,128]{1,0:T(8,128)(2,1)}, bf16[128,128]{1,0:T(8,128)(2,1)}, f32[160,2,128]{2,1,0:T(2,128)}) custom-call(bf16[128,1024]{1,0:T(8,128)(2,1)} %get-tuple-element.12.q_ref, bf16[128,128]{1,0:T(8,128)(2,1)} %get-tuple-element.13.k_ref, bf16[128,128]{1,0:T(8,128)(2,1)} %get-tuple-element.14.v_ref, ...), custom_call_target="tpu_custom_call" | custom-call | tf_op jit(solution)/shard_map/pallas_call | solution.py:353

commit v3 on v2

--- a/solution.py
+++ b/solution.py
@@ -14,13 +14,12 @@
 NY = 4
 NH = 8
 GROUP = 8
-WIN = 640
+WIN = 1280
 ROWS = 160
 BACK = 4
 KEYS = (BACK + 1) * BLK
 NEG = -1e30
-PLACE = (0, 1, 3, 5, 7, 6, 4, 2)
-ORDER = (4, 3, 5, 2, 6, 1, 7)
+TERMS = 4
 SCALE = 1.0 / math.sqrt(HD)
 MESH = pl.DeviceIdType.MESH
 
@@ -42,6 +41,8 @@
     d = lax.axis_index("dp")
     z, xl = c // 2, c % 2
     xh, y = h // NY, h % NY
+    side = z % 2
+    way = 1 - 2 * side
 
     def ctx(delta):
         return {"ctx": (c + delta + NCTX) % NCTX}
@@ -52,11 +53,14 @@
     def head(dx, dy):
         return {"head": head_index(dx, dy)}
 
+    core_peer = {"dp": 1 - d}
+    side_peer = {"ctx": c + 2 * way}
     x_peer = {"ctx": c + 1 - 2 * xl}
-    core_peer = {"dp": 1 - d}
+    far_peer = {"ctx": c + 2 * way + 1 - 2 * xl}
+    reach = {1: -way, 2: 2 * way, 3: -3 * way}
 
     barrier = pltpu.get_barrier_semaphore()
-    peers = [ctx(s) for s in (1, 2, 3, 4, -1, -2, -3, -4, 6, -6, 8)]
+    peers = [ctx(s) for s in (1, 2, 3, 4, -1, -2, -3, -4)] + [ctx(-6 * way)]
     peers += [head(1, 0), head(0, 1), head(0, 2), head(0, 3), core_peer]
     for peer in peers:
         pl.semaphore_signal(barrier, inc=1, device_id=peer, device_id_type=MESH)
@@ -106,8 +110,7 @@
 
     for copy in local:
         copy.wait()
-    window = xbuf[:, pl.ds(pl.multiple_of(z * WIN, 128), WIN)]
-    xall[0, h] = window
+    xall[0, h] = xbuf[:, pl.ds(pl.multiple_of((z // 2) * WIN, 128), WIN)]
     pl.semaphore_wait(barrier, len(peers))
 
     def push(src, dst, send, recv, peer):
@@ -118,32 +121,66 @@
         copy.start()
         return copy
 
-    a_copies = []
-    for kind, held in enumerate((kall, vall)):
-        for j in range(BACK, 0, -1):
-            a_copies.append(
-                push(
-                    held.at[pl.ds(0, BLK)], held.at[pl.ds(j * BLK, BLK)],
-                    a_send.at[kind, j - 1], a_recv.at[kind, j - 1], ctx(j),
-                )
-            )
+    a_copies = {}
+
+    def hand_on(kind, held, j, source, peer):
+        a_copies[kind, j] = push(
+            held.at[pl.ds(source, BLK)], held.at[pl.ds(j * BLK, BLK)],
+            a_send.at[kind, j - 1], a_recv.at[kind, j - 1], peer,
+        )
+
+    hand_on(0, kall, 4, 0, ctx(4))
+    hand_on(1, vall, 4, 0, ctx(4))
+    hand_on(0, kall, 2, 0, ctx(2))
+    hand_on(0, kall, 1, 0, ctx(1))
     x1_copies = []
-    for s in range(1, NZ):
-        there = (z + s) % NZ
-        x1_copies.append(
-            push(
-                xbuf.at[:, pl.ds(pl.multiple_of(there * WIN, 128), WIN)],
-                xall.at[PLACE[s], h], x1_send.at[s - 1], x1_recv.at[s - 1], ctx(2 * s),
-            )
-        )
-    x2_copies = []
-
-    def spread(at, peer):
-        i = len(x2_copies)
-        x2_copies.append(push(xall.at[:, at], xall.at[:, at], x2_send.at[i], x2_recv.at[i], peer))
-
-    for copy in a_copies[:BACK]:
-        copy.wait_recv()
+    for r in (3, 2, 1):
+        there = (z + reach[r] + NZ) % NZ // 2
+        copy = push(
+            xbuf.at[:, pl.ds(pl.multiple_of(there * WIN, 128), WIN)],
+            xall.at[r, h], x1_send.at[r - 1], x1_recv.at[r - 1], ctx(2 * reach[r]),
+        )
+        x1_copies.append((r, copy))
+    hand_on(1, vall, 2, 0, ctx(2))
+    hand_on(1, vall, 1, 0, ctx(1))
+    third = pl.multiple_of(xl * BACK * BLK, BLK)
+    third_peer = {"ctx": (c + 3 - 4 * xl + NCTX) % NCTX}
+    for kind, held in ((0, kall), (1, vall)):
+        a_copies[kind, 4].wait_recv()
+        hand_on(kind, held, 3, third, third_peer)
+    x2_copies = {}
+
+    def spread(step, group, at, peer):
+        part = xall.at[pl.ds(2 * group, 2), at]
+        x2_copies[step, group] = push(
+            part, part, x2_send.at[group, step], x2_recv.at[group, step], peer
+        )
+
+    def spread_own(group):
+        for copy in x1_copies:
+            if copy[0] // 2 == group:
+                copy[1].wait_recv()
+        spread(0, group, h, head(1, 0))
+        spread(1, group, h, head(0, 1))
+        spread(2, group, h, head(0, -1))
+
+    def spread_own_on(group):
+        x2_copies[1, group].wait_recv()
+        spread(3, group, head_index(0, -1), head(0, 1))
+
+    def spread_other(group):
+        x2_copies[0, group].wait_recv()
+        spread(4, group, head_index(1, 0), head(0, 1))
+        spread(5, group, head_index(1, 0), head(0, -1))
+
+    def spread_other_on(group):
+        x2_copies[5, group].wait_recv()
+        spread(6, group, head_index(1, 1), head(0, -1))
+
+    spread_own(0)
+    spread_own(1)
+    for j in (1, 2, 3):
+        a_copies[0, j].wait_recv()
 
     def weigh(p, carry):
         cols = pl.ds(pl.multiple_of(p * 2 * BLK, 2 * BLK), 2 * BLK)
@@ -171,14 +208,10 @@
         )
     own_v = dot(pbb[pl.ds(0, BLK), :], gbuf[...], ((1,), (0,)))
 
-    for copy in x1_copies:
-        copy.wait_recv()
-    spread(h, head(0, 1))
-    spread(h, head(0, -1))
-    spread(h, head(1, 0))
-
-    for copy in a_copies[BACK:]:
-        copy.wait_recv()
+    spread_own_on(0)
+
+    for j in (1, 2, 3):
+        a_copies[1, j].wait_recv()
 
     def differ(p, carry):
         cols = pl.ds(pl.multiple_of(p * 2 * BLK, 2 * BLK), 2 * BLK)
@@ -200,10 +233,11 @@
         )
     own_k = dot(dsb[pl.ds(0, BLK), :], qbuf[...], ((1,), (0,))) * SCALE
 
-    x2_copies[0].wait_recv()
-    spread(head_index(0, -1), head(0, 1))
-
-    d_copies = []
+    spread_other(0)
+    spread_own_on(1)
+    spread_other(1)
+
+    d_copies = {}
 
     def collect(kind, own, received, copies, held, out_ref):
         for copy in copies:
@@ -213,12 +247,10 @@
         final = own.astype(jnp.bfloat16)
         held[0] = final
         out_ref[...] = final
-        for s in ORDER:
-            d_copies.append(
-                push(
-                    held.at[0], held.at[PLACE[s]],
-                    d_send.at[kind, s - 1], d_recv.at[kind, s - 1], ctx(2 * s),
-                )
+        for r in (3, 2, 1):
+            d_copies[kind, r] = push(
+                held.at[0], held.at[r],
+                d_send.at[kind, r - 1], d_recv.at[kind, r - 1], ctx(2 * reach[r]),
             )
 
     collect(0, own_v, vrecv, c_copies[:BACK], gv, ov_ref)
@@ -232,50 +264,69 @@
 
     lax.fori_loop(0, GROUP // 2, query_grads, 0)
 
-    x2_copies[2].wait_recv()
-    spread(head_index(1, 0), head(0, 1))
-    spread(head_index(1, 0), head(0, -1))
+    spread_other_on(0)
+    spread_other_on(1)
 
     collect(1, own_k, krecv, c_copies[BACK:], gk, ok_ref)
 
-    x2_copies[5].wait_recv()
-    spread(head_index(1, 1), head(0, -1))
-    for i in (1, 3, 4, 6):
-        x2_copies[i].wait_recv()
-
-    for i in range(NZ):
-        xt[:, pl.ds(i * BLK, BLK)] = xall[i].reshape(BLK, WIN).T
+    for step in (2, 3, 4, 6):
+        for group in range(2):
+            x2_copies[step, group].wait_recv()
+
+    for r in range(TERMS):
+        xt[:, pl.ds(r * BLK, BLK)] = xall[r].reshape(BLK, WIN).T
 
     e_copies = []
 
-    def reduce_cores(kind, held, acc):
-        for copy in d_copies[kind * (NZ - 1) : (kind + 1) * (NZ - 1)]:
-            copy.wait_recv()
-        product = dot(xt[...], held[...].reshape(NZ * BLK, HD), ((1,), (0,)))
-        acc[...] = product.reshape(2, 2, ROWS, HD)
+    def product(kind, held, acc, first, last):
+        for r in range(max(first, 1), last):
+            d_copies[kind, r].wait_recv()
+        rows = held[first:last].reshape((last - first) * BLK, HD)
+        part = dot(xt[:, first * BLK : last * BLK], rows, ((1,), (0,)))
+        part = part.reshape(2, 2, 2, ROWS, HD)
+        acc[...] = part if first == 0 else acc[...] + part
+
+    def send_core(kind, acc):
         e_copies.append(
             push(
-                acc.at[:, 1 - d], e1.at[kind],
-                e_send.at[0, kind], e_recv.at[0, kind], core_peer,
+                acc.at[:, :, 1 - d], e1.at[kind],
+                e_send.at[kind, 0], e_recv.at[kind, 0], core_peer,
             )
         )
-        e_copies[-1].wait_recv()
-        u2[kind] = acc[1 - xl, d] + e1[kind, 1 - xl]
-        e_copies.append(
-            push(
-                u2.at[kind], e2.at[kind],
-                e_send.at[1, kind], e_recv.at[1, kind], x_peer,
+
+    def send_others(kind, acc):
+        e_copies[kind * 4].wait_recv()
+        parts = ((1 - side, 1 - xl, far_peer), (1 - side, xl, side_peer), (side, 1 - xl, x_peer))
+        for i, (at_side, at_x, peer) in enumerate(parts):
+            both = acc[at_side, at_x, d] + e1[kind, at_side, at_x]
+            u2[kind, i] = both.astype(jnp.bfloat16)
+            e_copies.append(
+                push(
+                    u2.at[kind, i], e2.at[kind, i],
+                    e_send.at[kind, i + 1], e_recv.at[kind, i + 1], peer,
+                )
             )
-        )
-
-    reduce_cores(0, gv, acc_v)
-    reduce_cores(1, gk, acc_k)
-    e_copies[1].wait_recv()
-    ow_ref[1] = acc_v[xl, d] + e1[0, xl] + e2[0]
-    e_copies[3].wait_recv()
-    ow_ref[0] = acc_k[xl, d] + e1[1, xl] + e2[1]
-
-    for copy in a_copies + x1_copies + x2_copies + c_copies + d_copies + e_copies:
+
+    def total(kind, acc):
+        whole = acc[side, xl, d] + e1[kind, side, xl]
+        for i in range(3):
+            e_copies[kind * 4 + i + 1].wait_recv()
+            whole = whole + e2[kind, i].astype(jnp.float32)
+        return whole
+
+    product(0, gv, acc_v, 0, TERMS)
+    send_core(0, acc_v)
+    product(1, gk, acc_k, 0, TERMS - 1)
+    send_others(0, acc_v)
+    product(1, gk, acc_k, TERMS - 1, TERMS)
+    send_core(1, acc_k)
+    send_others(1, acc_k)
+    ow_ref[1] = total(0, acc_v)
+    ow_ref[0] = total(1, acc_k)
+
+    for copy in list(a_copies.values()) + list(d_copies.values()) + c_copies + e_copies:
+        copy.wait_send()
+    for copy in [copy for _, copy in x1_copies] + list(x2_copies.values()):
         copy.wait_send()
 
 
@@ -306,7 +357,7 @@
         scratch_shapes=[
             pltpu.VMEM((GROUP * BLK, HD), bf16),
             pltpu.VMEM((GROUP * BLK, HD), bf16),
-            pltpu.VMEM((BLK // NH, NZ * WIN), bf16),
+            pltpu.VMEM((BLK // NH, TERMS * WIN), bf16),
             pltpu.VMEM((KEYS, HD), bf16),
             pltpu.VMEM((KEYS, HD), bf16),
             pltpu.VMEM((KEYS, BLK), f32),
@@ -317,28 +368,28 @@
             pltpu.VMEM((BACK, BLK, HD), bf16),
             pltpu.VMEM((BACK, BLK, HD), bf16),
             pltpu.VMEM((BACK, BLK, HD), bf16),
-            pltpu.VMEM((NZ, NH, BLK // NH, WIN), bf16),
-            pltpu.VMEM((WIN, NZ * BLK), bf16),
-            pltpu.VMEM((NZ, BLK, HD), bf16),
-            pltpu.VMEM((NZ, BLK, HD), bf16),
-            pltpu.VMEM((2, 2, ROWS, HD), f32),
-            pltpu.VMEM((2, 2, ROWS, HD), f32),
-            pltpu.VMEM((2, 2, ROWS, HD), f32),
-            pltpu.VMEM((2, ROWS, HD), f32),
-            pltpu.VMEM((2, ROWS, HD), f32),
+            pltpu.VMEM((TERMS, NH, BLK // NH, WIN), bf16),
+            pltpu.VMEM((WIN, TERMS * BLK), bf16),
+            pltpu.VMEM((TERMS, BLK, HD), bf16),
+            pltpu.VMEM((TERMS, BLK, HD), bf16),
+            pltpu.VMEM((2, 2, 2, ROWS, HD), f32),
+            pltpu.VMEM((2, 2, 2, ROWS, HD), f32),
+            pltpu.VMEM((2, 2, 2, ROWS, HD), f32),
+            pltpu.VMEM((2, 3, ROWS, HD), bf16),
+            pltpu.VMEM((2, 3, ROWS, HD), bf16),
             dma((2 * GROUP + 3,)),
             dma((2, BACK)),
             dma((2, BACK)),
-            dma((NZ - 1,)),
-            dma((NZ - 1,)),
-            dma((7,)),
-            dma((7,)),
+            dma((TERMS - 1,)),
+            dma((TERMS - 1,)),
+            dma((2, 7)),
+            dma((2, 7)),
             dma((2, BACK)),
             dma((2, BACK)),
-            dma((2, NZ - 1)),
-            dma((2, NZ - 1)),
-            dma((2, 2)),
-            dma((2, 2)),
+            dma((2, TERMS - 1)),
+            dma((2, TERMS - 1)),
+            dma((2, 4)),
+            dma((2, 4)),
         ],
         compiler_params=pltpu.CompilerParams(
             collective_id=0, has_side_effects=True, vmem_limit_bytes=60 * 1024 * 1024

time: 52.4 us -> 48.3 us (0.922); the launches traced: 52.3 us -> 47.6 us
  Pallas kernels: 51.6 us -> 47 us
    pallas_call x1, Pallas kernels: 49.8 us -> 45.1 us  [local(): pl.pallas_call(kernel, out_shape=[jax.ShapeDtypeStruct((BLK, GROUP * HD),...]
where the time goes in v3:
time: 48.3 us; the launch traced here: 47.6 us
  Pallas kernels  47 us (97%)
  between operations  0.64 us (1%)
    pallas_call x1, Pallas kernels, local(): pl.pallas_call(kernel, out_shape=[jax.ShapeDtypeStruct((BLK, GROUP * HD),...  45.1 us
    pallas_call x1, Pallas kernels, local(): pl.pallas_call(finish, out_shape=[jax.ShapeDtypeStruct((BLK, GROUP * HD),...  1.82 us

profile of v3, /device:TPU:1, one launch (start us, length us, event | category | flops | bytes accessed | tf_op | source)
XLA Modules:
  0.0 47.6 jit_solution(12617076828114774442)
XLA Ops:
  0.6 45.1 %shard_map.111 = (bf16[128,1024]{1,0:T(8,128)(2,1)}, bf16[128,128]{1,0:T(8,128)(2,1)}, bf16[128,128]{1,0:T(8,128)(2,1)}, f32[2,160,128]{2,1,0:T(8,128)}) custom-call(bf16[128,1024]{1,0:T(8,128)(2,1)} %bitcast.8, bf16[128,128]{1,0:T(8,128)(2,1)} %bitcast.12, bf16[128,128]{1,0:T(8,128)(2,1)} %bitcast.13, bf16[128,1024]{1,0:T(8,128)(2,1)} %bitcast.9, ...), custom_call_target="tpu_custom_call" | custom-call | flops 1300000000 | bytes 2000000 | tf_op jit(solution)/shard_map/pallas_call | solution.py:347
  45.8 1.8 %shard_map.112 = (bf16[128,1024]{1,0:T(8,128)(2,1)}, bf16[128,128]{1,0:T(8,128)(2,1)}, bf16[128,128]{1,0:T(8,128)(2,1)}, f32[160,2,128]{2,1,0:T(2,128)}) custom-call(bf16[128,1024]{1,0:T(8,128)(2,1)} %get-tuple-element.12.q_ref, bf16[128,128]{1,0:T(8,128)(2,1)} %get-tuple-element.13.k_ref, bf16[128,128]{1,0:T(8,128)(2,1)} %get-tuple-element.14.v_ref, ...), custom_call_target="tpu_custom_call" | custom-call | tf_op jit(solution)/shard_map/pallas_call | solution.py:404

commit v4 on v3

--- a/solution.py
+++ b/solution.py
@@ -347,10 +347,10 @@
     grad_q, grad_k, grad_v, grad_w = pl.pallas_call(
         kernel,
         out_shape=[
-            jax.ShapeDtypeStruct((BLK, GROUP * HD), bf16),
-            jax.ShapeDtypeStruct((BLK, HD), bf16),
-            jax.ShapeDtypeStruct((BLK, HD), bf16),
-            jax.ShapeDtypeStruct((2, ROWS, HD), f32),
+            pltpu.VMEM((BLK, GROUP * HD), bf16),
+            pltpu.VMEM((BLK, HD), bf16),
+            pltpu.VMEM((BLK, HD), bf16),
+            pltpu.VMEM((2, ROWS, HD), f32),
         ],
         in_specs=[hbm] * 5 + [vmem, smem, smem],
         out_specs=[vmem] * 4,
@@ -411,6 +411,7 @@
         ],
         in_specs=[vmem] * 4,
         out_specs=[vmem] * 4,
+        compiler_params=pltpu.CompilerParams(vmem_limit_bytes=4 * 1024 * 1024),
     )(grad_q, grad_k, grad_v, grad_w)
     return (grad_q[None], grad_k[None], grad_v[None], grad_w)
 

time: 48.3 us -> 46.4 us (0.961)
  Pallas kernels: 47 us -> 45.1 us
    pallas_call x1, Pallas kernels: 1.82 us -> 0.8 us  [local(): pl.pallas_call(finish, out_shape=[jax.ShapeDtypeStruct((BLK, GROUP * HD),...]
    pallas_call x1, Pallas kernels: 45.1 us -> 44.3 us  [local(): pl.pallas_call(kernel, out_shape=[pltpu.VMEM((BLK, GROUP * HD), bf16), pl...]
where the time goes in v4:
time: 46.4 us; the launch traced here: 45.8 us
  Pallas kernels  45.1 us (97%)
  between operations  0.64 us (1%)
    pallas_call x1, Pallas kernels, local(): pl.pallas_call(kernel, out_shape=[pltpu.VMEM((BLK, GROUP * HD), bf16), pl...  44.3 us

profile of v4, /device:TPU:1, one launch (start us, length us, event | category | flops | bytes accessed | tf_op | source)
XLA Modules:
  0.0 45.8 jit_solution(2115615756928546733)
XLA Ops:
  0.6 44.3 %shard_map.111 = (bf16[128,1024]{1,0:T(8,128)(2,1)S(1)}, bf16[128,128]{1,0:T(8,128)(2,1)S(1)}, bf16[128,128]{1,0:T(8,128)(2,1)S(1)}, f32[2,160,128]{2,1,0:T(8,128)S(1)}) custom-call(bf16[128,1024]{1,0:T(8,128)(2,1)} %bitcast.8, bf16[128,128]{1,0:T(8,128)(2,1)} %bitcast.12, bf16[128,128]{1,0:T(8,128)(2,1)} %bitcast.13, bf16[128,1024]{1,0:T(8,128)(2,1)} %bitcast.9, ...), custom_call_target="tpu_custom_call" | custom-call | flops 1300000000 | bytes 2000000 | tf_op jit(solution)/shard_map/pallas_call | solution.py:347
  45.0 0.8 %shard_map.112 = (bf16[128,1024]{1,0:T(8,128)(2,1)}, bf16[128,128]{1,0:T(8,128)(2,1)}, bf16[128,128]{1,0:T(8,128)(2,1)}, f32[160,2,128]{2,1,0:T(2,128)}) custom-call(bf16[128,1024]{1,0:T(8,128)(2,1)S(1)} %get-tuple-element.12.q_ref, bf16[128,128]{1,0:T(8,128)(2,1)S(1)} %get-tuple-element.13.k_ref, bf16[128,128]{1,0:T(8,128)(2,1)S(1)} %get-tuple-element.14.v_ref, ...), custom_call_target="tpu_custom_call" | custom-call | tf_op jit(solution)/shard_map/pallas_call | solution.py:404

commit v5 on v4

--- a/solution.py
+++ b/solution.py
@@ -31,7 +31,7 @@
 def kernel(
     q_hbm, k_hbm, v_hbm, g_hbm, x_hbm, doc_ref, rank_ref, take_ref,
     oq_ref, ok_ref, ov_ref, ow_ref,
-    qbuf, gbuf, xbuf, kall, vall, bias, probs, dsb, pbb, vsend, vrecv, ksend, krecv,
+    qbuf, gbuf, xbuf, kall, vall, bias, probs, pushes, dsb, pbb, vsend, vrecv, ksend, krecv,
     xall, xt, gv, gk, acc_v, acc_k, e1, u2, e2,
     loc_sem, a_send, a_recv, x1_send, x1_recv, x2_send, x2_recv,
     c_send, c_recv, d_send, d_recv, e_send, e_recv,
@@ -111,6 +111,26 @@
     for copy in local:
         copy.wait()
     xall[0, h] = xbuf[:, pl.ds(pl.multiple_of((z // 2) * WIN, 128), WIN)]
+
+    chunks = [pl.ds(p * 2 * BLK, 2 * BLK) for p in range(GROUP // 2)]
+    tops = [jnp.full((1, 2 * BLK), NEG, jnp.float32) for _ in chunks]
+
+    def score(first, last):
+        rows = pl.ds(first * BLK, (last - first) * BLK)
+        hidden = bias[rows, :]
+        hidden = jnp.concatenate([hidden, hidden], 1)
+        for p, cols in enumerate(chunks):
+            part = dot(kall[rows, :], qbuf[cols, :], ((1,), (1,))) * SCALE + hidden
+            probs[rows, cols] = part
+            tops[p] = jnp.maximum(tops[p], jnp.max(part, 0, keepdims=True))
+
+    def value_products(first, last):
+        rows = pl.ds(first * BLK, (last - first) * BLK)
+        for cols in chunks:
+            pushes[rows, cols] = dot(vall[rows, :], gbuf[cols, :], ((1,), (1,)))
+
+    score(0, 1)
+    value_products(0, 1)
     pl.semaphore_wait(barrier, len(peers))
 
     def push(src, dst, send, recv, peer):
@@ -148,6 +168,8 @@
     for kind, held in ((0, kall), (1, vall)):
         a_copies[kind, 4].wait_recv()
         hand_on(kind, held, 3, third, third_peer)
+    score(4, 5)
+    value_products(4, 5)
     x2_copies = {}
 
     def spread(step, group, at, peer):
@@ -179,59 +201,56 @@
 
     spread_own(0)
     spread_own(1)
-    for j in (1, 2, 3):
+    for j in (1, 2):
         a_copies[0, j].wait_recv()
-
-    def weigh(p, carry):
-        cols = pl.ds(pl.multiple_of(p * 2 * BLK, 2 * BLK), 2 * BLK)
-        hidden = bias[...]
-        scores = dot(kall[...], qbuf[cols, :], ((1,), (1,))) * SCALE
-        scores = scores + jnp.concatenate([hidden, hidden], 1)
-        top = jnp.max(scores, 0, keepdims=True)
-        weights = jnp.exp(scores - top)
-        total = jnp.sum(weights, 0, keepdims=True)
-        share = weights * (1.0 / total)
-        probs[:, cols] = share
-        pbb[:, cols] = share.astype(jnp.bfloat16)
-        return carry
-
-    lax.fori_loop(0, GROUP // 2, weigh, 0)
+    score(1, 3)
+    a_copies[0, 3].wait_recv()
+    score(3, 4)
+
+    inverse = []
+    for p, cols in enumerate(chunks):
+        weights = jnp.exp(probs[:, cols] - tops[p])
+        probs[:, cols] = weights
+        inverse.append(1.0 / jnp.sum(weights, 0, keepdims=True))
+    inverse = jnp.concatenate(inverse, 1)
     c_copies = []
-    for j in range(BACK, 0, -1):
-        grad_v = dot(pbb[pl.ds(j * BLK, BLK), :], gbuf[...], ((1,), (0,)))
-        vsend[j - 1] = grad_v.astype(jnp.bfloat16)
+
+    def send_back(kind, j, held, received, grad):
+        held[j - 1] = grad.astype(jnp.bfloat16)
         c_copies.append(
             push(
-                vsend.at[j - 1], vrecv.at[j - 1],
-                c_send.at[0, j - 1], c_recv.at[0, j - 1], ctx(-j),
+                held.at[j - 1], received.at[j - 1],
+                c_send.at[kind, j - 1], c_recv.at[kind, j - 1], ctx(-j),
             )
         )
-    own_v = dot(pbb[pl.ds(0, BLK), :], gbuf[...], ((1,), (0,)))
+
+    for j in range(BACK, -1, -1):
+        rows = pl.ds(j * BLK, BLK)
+        share = probs[rows, :] * inverse
+        probs[rows, :] = share
+        pbb[rows, :] = share.astype(jnp.bfloat16)
+        own_v = dot(pbb[rows, :], gbuf[...], ((1,), (0,)))
+        if j > 0:
+            send_back(0, j, vsend, vrecv, own_v)
 
     spread_own_on(0)
 
-    for j in (1, 2, 3):
+    for j in (1, 2):
         a_copies[1, j].wait_recv()
-
-    def differ(p, carry):
-        cols = pl.ds(pl.multiple_of(p * 2 * BLK, 2 * BLK), 2 * BLK)
-        pushes = dot(vall[...], gbuf[cols, :], ((1,), (1,)))
-        share = probs[:, cols]
-        delta = jnp.sum(share * pushes, 0, keepdims=True)
-        dsb[:, cols] = (share * (pushes - delta)).astype(jnp.bfloat16)
-        return carry
-
-    lax.fori_loop(0, GROUP // 2, differ, 0)
-    for j in range(BACK, 0, -1):
-        grad_k = dot(dsb[pl.ds(j * BLK, BLK), :], qbuf[...], ((1,), (0,))) * SCALE
-        ksend[j - 1] = grad_k.astype(jnp.bfloat16)
-        c_copies.append(
-            push(
-                ksend.at[j - 1], krecv.at[j - 1],
-                c_send.at[1, j - 1], c_recv.at[1, j - 1], ctx(-j),
-            )
-        )
-    own_k = dot(dsb[pl.ds(0, BLK), :], qbuf[...], ((1,), (0,))) * SCALE
+    value_products(1, 3)
+    a_copies[1, 3].wait_recv()
+    value_products(3, 4)
+    delta = [
+        jnp.sum(probs[:, cols] * pushes[:, cols], 0, keepdims=True) for cols in chunks
+    ]
+    delta = jnp.concatenate(delta, 1)
+    for j in range(BACK, -1, -1):
+        rows = pl.ds(j * BLK, BLK)
+        change = probs[rows, :] * (pushes[rows, :] - delta)
+        dsb[rows, :] = change.astype(jnp.bfloat16)
+        own_k = dot(dsb[rows, :], qbuf[...], ((1,), (0,))) * SCALE
+        if j > 0:
+            send_back(1, j, ksend, krecv, own_k)
 
     spread_other(0)
     spread_own_on(1)
@@ -361,6 +380,7 @@
             pltpu.VMEM((KEYS, HD), bf16),
             pltpu.VMEM((KEYS, HD), bf16),
             pltpu.VMEM((KEYS, BLK), f32),
+            pltpu.VMEM((KEYS, GROUP * BLK), f32),
             pltpu.VMEM((KEYS, GROUP * BLK), f32),
             pltpu.VMEM((KEYS, GROUP * BLK), bf16),
             pltpu.VMEM((KEYS, GROUP * BLK), bf16),

time: 46.4 us -> 44.8 us (0.966)
  Pallas kernels: 45.1 us -> 44 us
    pallas_call x1, Pallas kernels: 44.3 us -> 43.2 us  [local(): pl.pallas_call(kernel, out_shape=[pltpu.VMEM((BLK, GROUP * HD), bf16), pl...]
where the time goes in v5:
time: 44.8 us; the launch traced here: 44.6 us
  Pallas kernels  44 us (98%)
  between operations  0.64 us (1%)
    pallas_call x1, Pallas kernels, local(): pl.pallas_call(kernel, out_shape=[pltpu.VMEM((BLK, GROUP * HD), bf16), pl...  43.2 us

profile of v5, /device:TPU:1, one launch (start us, length us, event | category | flops | bytes accessed | tf_op | source)
XLA Modules:
  0.0 44.6 jit_solution(14159264182798998244)
XLA Ops:
  0.6 43.2 %shard_map.111 = (bf16[128,1024]{1,0:T(8,128)(2,1)S(1)}, bf16[128,128]{1,0:T(8,128)(2,1)S(1)}, bf16[128,128]{1,0:T(8,128)(2,1)S(1)}, f32[2,160,128]{2,1,0:T(8,128)S(1)}) custom-call(bf16[128,1024]{1,0:T(8,128)(2,1)} %bitcast.8, bf16[128,128]{1,0:T(8,128)(2,1)} %bitcast.12, bf16[128,128]{1,0:T(8,128)(2,1)} %bitcast.13, bf16[128,1024]{1,0:T(8,128)(2,1)} %bitcast.9, ...), custom_call_target="tpu_custom_call" | custom-call | flops 1300000000 | bytes 2000000 | tf_op jit(solution)/shard_map/pallas_call | solution.py:366
  43.8 0.8 %shard_map.112 = (bf16[128,1024]{1,0:T(8,128)(2,1)}, bf16[128,128]{1,0:T(8,128)(2,1)}, bf16[128,128]{1,0:T(8,128)(2,1)}, f32[160,2,128]{2,1,0:T(2,128)}) custom-call(bf16[128,1024]{1,0:T(8,128)(2,1)S(1)} %get-tuple-element.12.q_ref, bf16[128,128]{1,0:T(8,128)(2,1)S(1)} %get-tuple-element.13.k_ref, bf16[128,128]{1,0:T(8,128)(2,1)S(1)} %get-tuple-element.14.v_ref, ...), custom_call_target="tpu_custom_call" | custom-call | tf_op jit(solution)/shard_map/pallas_call | solution.py:424

commit v6 on v5

--- a/solution.py
+++ b/solution.py
@@ -20,6 +20,7 @@
 KEYS = (BACK + 1) * BLK
 NEG = -1e30
 TERMS = 4
+PARTS = ((0, 2), (2, 4))
 SCALE = 1.0 / math.sqrt(HD)
 MESH = pl.DeviceIdType.MESH
 
@@ -173,14 +174,15 @@
     x2_copies = {}
 
     def spread(step, group, at, peer):
-        part = xall.at[pl.ds(2 * group, 2), at]
+        first, last = PARTS[group]
+        part = xall.at[pl.ds(first, last - first), at]
         x2_copies[step, group] = push(
             part, part, x2_send.at[group, step], x2_recv.at[group, step], peer
         )
 
     def spread_own(group):
         for copy in x1_copies:
-            if copy[0] // 2 == group:
+            if PARTS[group][0] <= copy[0] < PARTS[group][1]:
                 copy[1].wait_recv()
         spread(0, group, h, head(1, 0))
         spread(1, group, h, head(0, 1))
@@ -224,7 +226,7 @@
             )
         )
 
-    for j in range(BACK, -1, -1):
+    for j in (1, 3, 2, 4, 0):
         rows = pl.ds(j * BLK, BLK)
         share = probs[rows, :] * inverse
         probs[rows, :] = share
@@ -244,7 +246,7 @@
         jnp.sum(probs[:, cols] * pushes[:, cols], 0, keepdims=True) for cols in chunks
     ]
     delta = jnp.concatenate(delta, 1)
-    for j in range(BACK, -1, -1):
+    for j in (1, 3, 2, 4, 0):
         rows = pl.ds(j * BLK, BLK)
         change = probs[rows, :] * (pushes[rows, :] - delta)
         dsb[rows, :] = change.astype(jnp.bfloat16)
@@ -253,8 +255,8 @@
             send_back(1, j, ksend, krecv, own_k)
 
     spread_other(0)
+    spread_other(1)
     spread_own_on(1)
-    spread_other(1)
 
     d_copies = {}
 
@@ -288,62 +290,70 @@
 
     collect(1, own_k, krecv, c_copies[BACK:], gk, ok_ref)
 
-    for step in (2, 3, 4, 6):
-        for group in range(2):
+    def flip(group):
+        for step in (2, 3, 4, 6):
             x2_copies[step, group].wait_recv()
-
-    for r in range(TERMS):
-        xt[:, pl.ds(r * BLK, BLK)] = xall[r].reshape(BLK, WIN).T
-
-    e_copies = []
-
-    def product(kind, held, acc, first, last):
+        for r in range(*PARTS[group]):
+            xt[:, pl.ds(r * BLK, BLK)] = xall[r].reshape(BLK, WIN).T
+
+    e_copies = {}
+
+    def product(kind, held, acc, at_side, first, last):
         for r in range(max(first, 1), last):
-            d_copies[kind, r].wait_recv()
-        rows = held[first:last].reshape((last - first) * BLK, HD)
-        part = dot(xt[:, first * BLK : last * BLK], rows, ((1,), (0,)))
-        part = part.reshape(2, 2, 2, ROWS, HD)
-        acc[...] = part if first == 0 else acc[...] + part
-
-    def send_core(kind, acc):
-        e_copies.append(
-            push(
-                acc.at[:, :, 1 - d], e1.at[kind],
-                e_send.at[kind, 0], e_recv.at[kind, 0], core_peer,
-            )
-        )
+            if (kind, r) not in landed:
+                landed.add((kind, r))
+                d_copies[kind, r].wait_recv()
+        rows = pl.ds(pl.multiple_of(at_side * (WIN // 2), 128), WIN // 2)
+        terms = held[first:last].reshape((last - first) * BLK, HD)
+        part = dot(xt[rows, first * BLK : last * BLK], terms, ((1,), (0,)))
+        part = part.reshape(2, 2, ROWS, HD)
+        acc[at_side] = part if first == 0 else acc[at_side] + part
+
+    landed = set()
+
+    def exchange(kind, i, src, dst, peer):
+        e_copies[kind, i] = push(src, dst, e_send.at[kind, i], e_recv.at[kind, i], peer)
+
+    def send_core(kind, acc, i, at_side):
+        exchange(kind, i, acc.at[at_side, :, 1 - d], e1.at[kind, at_side], core_peer)
+
+    def send_other(kind, acc, i, at_side, at_x, peer):
+        both = acc[at_side, at_x, d] + e1[kind, at_side, at_x]
+        u2[kind, i] = both.astype(jnp.bfloat16)
+        exchange(kind, i + 2, u2.at[kind, i], e2.at[kind, i], peer)
 
     def send_others(kind, acc):
-        e_copies[kind * 4].wait_recv()
-        parts = ((1 - side, 1 - xl, far_peer), (1 - side, xl, side_peer), (side, 1 - xl, x_peer))
-        for i, (at_side, at_x, peer) in enumerate(parts):
-            both = acc[at_side, at_x, d] + e1[kind, at_side, at_x]
-            u2[kind, i] = both.astype(jnp.bfloat16)
-            e_copies.append(
-                push(
-                    u2.at[kind, i], e2.at[kind, i],
-                    e_send.at[kind, i + 1], e_recv.at[kind, i + 1], peer,
-                )
-            )
+        e_copies[kind, 0].wait_recv()
+        send_other(kind, acc, 0, 1 - side, 1 - xl, far_peer)
+        send_other(kind, acc, 1, 1 - side, xl, side_peer)
+        e_copies[kind, 1].wait_recv()
+        send_other(kind, acc, 2, side, 1 - xl, x_peer)
 
     def total(kind, acc):
         whole = acc[side, xl, d] + e1[kind, side, xl]
         for i in range(3):
-            e_copies[kind * 4 + i + 1].wait_recv()
+            e_copies[kind, i + 2].wait_recv()
             whole = whole + e2[kind, i].astype(jnp.float32)
         return whole
 
-    product(0, gv, acc_v, 0, TERMS)
-    send_core(0, acc_v)
-    product(1, gk, acc_k, 0, TERMS - 1)
+    flip(0)
+    for at_side in (1 - side, side):
+        product(0, gv, acc_v, at_side, 0, 2)
+    flip(1)
+    for i, at_side in enumerate((1 - side, side)):
+        product(0, gv, acc_v, at_side, 2, TERMS)
+        send_core(0, acc_v, i, at_side)
+    for at_side in (1 - side, side):
+        product(1, gk, acc_k, at_side, 0, TERMS - 1)
     send_others(0, acc_v)
-    product(1, gk, acc_k, TERMS - 1, TERMS)
-    send_core(1, acc_k)
+    for i, at_side in enumerate((1 - side, side)):
+        product(1, gk, acc_k, at_side, TERMS - 1, TERMS)
+        send_core(1, acc_k, i, at_side)
     send_others(1, acc_k)
     ow_ref[1] = total(0, acc_v)
     ow_ref[0] = total(1, acc_k)
 
-    for copy in list(a_copies.values()) + list(d_copies.values()) + c_copies + e_copies:
+    for copy in list(a_copies.values()) + list(d_copies.values()) + c_copies + list(e_copies.values()):
         copy.wait_send()
     for copy in [copy for _, copy in x1_copies] + list(x2_copies.values()):
         copy.wait_send()
@@ -402,14 +412,14 @@
             dma((2, BACK)),
             dma((TERMS - 1,)),
             dma((TERMS - 1,)),
-            dma((2, 7)),
-            dma((2, 7)),
+            dma((len(PARTS), 7)),
+            dma((len(PARTS), 7)),
             dma((2, BACK)),
             dma((2, BACK)),
             dma((2, TERMS - 1)),
             dma((2, TERMS - 1)),
-            dma((2, 4)),
-            dma((2, 4)),
+            dma((2, 5)),
+            dma((2, 5)),
         ],
         compiler_params=pltpu.CompilerParams(
             collective_id=0, has_side_effects=True, vmem_limit_bytes=60 * 1024 * 1024

time: 44.8 us -> 44.2 us (0.987)
  Pallas kernels: 44 us -> 43.4 us
    pallas_call x1, Pallas kernels: 43.2 us -> 42.6 us  [local(): pl.pallas_call(kernel, out_shape=[pltpu.VMEM((BLK, GROUP * HD), bf16), pl...]
where the time goes in v6:
time: 44.2 us; the launch traced here: 44.1 us
  Pallas kernels  43.4 us (98%)
  between operations  0.64 us (1%)
    pallas_call x1, Pallas kernels, local(): pl.pallas_call(kernel, out_shape=[pltpu.VMEM((BLK, GROUP * HD), bf16), pl...  42.6 us

profile of v6, /device:TPU:1, one launch (start us, length us, event | category | flops | bytes accessed | tf_op | source)
XLA Modules:
  0.0 44.1 jit_solution(10159373094013224793)
XLA Ops:
  0.6 42.6 %shard_map.111 = (bf16[128,1024]{1,0:T(8,128)(2,1)S(1)}, bf16[128,128]{1,0:T(8,128)(2,1)S(1)}, bf16[128,128]{1,0:T(8,128)(2,1)S(1)}, f32[2,160,128]{2,1,0:T(8,128)S(1)}) custom-call(bf16[128,1024]{1,0:T(8,128)(2,1)} %bitcast.8, bf16[128,128]{1,0:T(8,128)(2,1)} %bitcast.12, bf16[128,128]{1,0:T(8,128)(2,1)} %bitcast.13, bf16[128,1024]{1,0:T(8,128)(2,1)} %bitcast.9, ...), custom_call_target="tpu_custom_call" | custom-call | flops 1300000000 | bytes 2000000 | tf_op jit(solution)/shard_map/pallas_call | solution.py:376
  43.3 0.8 %shard_map.112 = (bf16[128,1024]{1,0:T(8,128)(2,1)}, bf16[128,128]{1,0:T(8,128)(2,1)}, bf16[128,128]{1,0:T(8,128)(2,1)}, f32[160,2,128]{2,1,0:T(2,128)}) custom-call(bf16[128,1024]{1,0:T(8,128)(2,1)S(1)} %get-tuple-element.12.q_ref, bf16[128,128]{1,0:T(8,128)(2,1)S(1)} %get-tuple-element.13.k_ref, bf16[128,128]{1,0:T(8,128)(2,1)S(1)} %get-tuple-element.14.v_ref, ...), custom_call_target="tpu_custom_call" | custom-call | tf_op jit(solution)/shard_map/pallas_call | solution.py:434

commit v7 on v6

--- a/solution.py
+++ b/solution.py
@@ -184,9 +184,9 @@
         for copy in x1_copies:
             if PARTS[group][0] <= copy[0] < PARTS[group][1]:
                 copy[1].wait_recv()
-        spread(0, group, h, head(1, 0))
         spread(1, group, h, head(0, 1))
         spread(2, group, h, head(0, -1))
+        spread(0, group, h, head(1, 0))
 
     def spread_own_on(group):
         x2_copies[1, group].wait_recv()

time: 44.2 us -> 44.2 us (level)
  no operation moved by 1% of the time
where the time goes in v7:
time: 44.2 us; the launch traced here: 44.1 us
  Pallas kernels  43.4 us (98%)
  between operations  0.64 us (1%)
    pallas_call x1, Pallas kernels, local(): pl.pallas_call(kernel, out_shape=[pltpu.VMEM((BLK, GROUP * HD), bf16), pl...  42.6 us

profile of v7, /device:TPU:1, one launch (start us, length us, event | category | flops | bytes accessed | tf_op | source)
XLA Modules:
  0.0 44.1 jit_solution(11166460487137670282)
XLA Ops:
  0.6 42.6 %shard_map.111 = (bf16[128,1024]{1,0:T(8,128)(2,1)S(1)}, bf16[128,128]{1,0:T(8,128)(2,1)S(1)}, bf16[128,128]{1,0:T(8,128)(2,1)S(1)}, f32[2,160,128]{2,1,0:T(8,128)S(1)}) custom-call(bf16[128,1024]{1,0:T(8,128)(2,1)} %bitcast.8, bf16[128,128]{1,0:T(8,128)(2,1)} %bitcast.12, bf16[128,128]{1,0:T(8,128)(2,1)} %bitcast.13, bf16[128,1024]{1,0:T(8,128)(2,1)} %bitcast.9, ...), custom_call_target="tpu_custom_call" | custom-call | flops 1300000000 | bytes 2000000 | tf_op jit(solution)/shard_map/pallas_call | solution.py:376
  43.3 0.8 %shard_map.112 = (bf16[128,1024]{1,0:T(8,128)(2,1)}, bf16[128,128]{1,0:T(8,128)(2,1)}, bf16[128,128]{1,0:T(8,128)(2,1)}, f32[160,2,128]{2,1,0:T(2,128)}) custom-call(bf16[128,1024]{1,0:T(8,128)(2,1)S(1)} %get-tuple-element.12.q_ref, bf16[128,128]{1,0:T(8,128)(2,1)S(1)} %get-tuple-element.13.k_ref, bf16[128,128]{1,0:T(8,128)(2,1)S(1)} %get-tuple-element.14.v_ref, ...), custom_call_target="tpu_custom_call" | custom-call | tf_op jit(solution)/shard_map/pallas_call | solution.py:434
